TPU v7x, 32 devices: a whole 2x2x4 slice. The times are simulated.
32 devices in a mesh: row: 4 (over z), col: 8 (over y, x, core).
Axes of the slice: x: 2, y: 2, z: 4, core: 2. Of those that a mesh axis runs over, the one named last changes fastest.
Arguments:
- recorded: bfloat16 [512, 64, 3072], P(('row', 'col')), may hold values from -6 to 6
- seg_count: int32 [32], P(('row', 'col')), may hold values from 0 to 16, as said below
- slot_station: int32 [512], P(('row', 'col')), may hold values from 0 to 255, as said below
- window_mask: int32 [256, 64], P(('row', 'col')), may hold values from 0 to 1, as said below
Outputs:
- cross_real: bfloat16 [256, 256, 384], P('row', 'col')
- cross_imag: bfloat16 [256, 256, 384], P('row', 'col')
Inputs may be any that keep to these rules, and one draw needn't show every extreme that they name: `seg_count`: recorder d = r * 8 + c serves row r of the grid; in every row exactly half of the 8 recorders have 16 live slots and the others none. `slot_station`: the live slots of the recorders of row r name each station of r * 64 to (r + 1) * 64 - 1 exactly once; a recorder's live slots name 2 or no stations of each owner (stations with equal s // 8); dead slots name arbitrary stations. `window_mask`: A station's invalid windows form one cyclic run of 0 to 64 windows.
All inputs are finite; a program needn't handle non-finite values.
Results may differ from a plain program's by a relative error of at most 0.0066.
Values may be sent and summed in bfloat16 or wider, within the bound.
A program may use at most 128 MiB of HBM per device.

v0:
```python
import math

import jax
import jax.numpy as jnp
from jax import lax
from jax.sharding import PartitionSpec as P

F = 384
L = 3072
F0 = 13
BAND = 64
CAP = 2
W = 64


def transform_table():
    times = jnp.arange(L, dtype=jnp.int32)
    freqs = jnp.arange(F, dtype=jnp.int32) + F0
    phase = times[:, None] * freqs[None, :] % L
    angle = phase.astype(jnp.float32) * (2.0 * math.pi / L)
    return jnp.concatenate([jnp.cos(angle), -jnp.sin(angle)], axis=1).astype(jnp.bfloat16)


def whiten(segments, table):
    count = segments.shape[0]
    spectrum = jnp.dot(segments.reshape(count * W, L), table, preferred_element_type=jnp.float32)
    real = spectrum[:, :F]
    imag = spectrum[:, F:]
    power = (real * real + imag * imag).reshape(count * W, F // BAND, BAND)
    factor = lax.rsqrt(jnp.mean(power, axis=2) + 1e-05)
    factor = jnp.repeat(factor, BAND, axis=1)
    white = jnp.concatenate([real * factor, imag * factor], axis=1)
    return white.astype(jnp.bfloat16).reshape(count, W, 2 * F)


def per_device(recorded, seg_count, slot_station, window_mask):
    columns = lax.axis_size("col")
    slots_here = recorded.shape[0]
    owned = window_mask.shape[0]
    outgoing = columns * CAP
    slot_index = jnp.arange(slots_here, dtype=jnp.int32)
    live = slot_index < seg_count[0]
    target_col = jnp.where(live, slot_station // owned % columns, columns)
    onehot = (target_col[:, None] == jnp.arange(columns, dtype=jnp.int32)[None, :]).astype(
        jnp.int32
    )
    earlier = jnp.cumsum(onehot, axis=0) - onehot
    rank = jnp.sum(earlier * onehot, axis=1)
    position = jnp.where(live, target_col * CAP + rank, outgoing)
    chosen = position[None, :] == jnp.arange(outgoing, dtype=jnp.int32)[:, None]
    source = jnp.sum(jnp.where(chosen, slot_index[None, :], 0), axis=1)
    local_id = jnp.sum(jnp.where(chosen, slot_station[None, :] % owned + 1, 0), axis=1) - 1
    labels = local_id.astype(jnp.bfloat16).reshape(columns, CAP)
    table = transform_table()
    payload = jnp.take(recorded, source, axis=0).reshape(columns, CAP, W, L)
    arrived, tags = (
        lax.all_to_all(payload, "col", split_axis=0, concat_axis=0, tiled=True),
        lax.all_to_all(labels, "col", split_axis=0, concat_axis=0, tiled=True),
    )
    tags = tags.reshape(outgoing).astype(jnp.int32)
    flat = arrived.reshape(outgoing, W, arrived.shape[3])
    match = tags[None, :] == jnp.arange(owned, dtype=jnp.int32)[:, None]
    pick = jnp.sum(jnp.where(match, jnp.arange(outgoing, dtype=jnp.int32)[None, :], 0), axis=1)
    mine = jnp.take(flat, pick, axis=0)
    spectra = whiten(mine, table)
    mask_float = window_mask.astype(jnp.bfloat16)
    spectra = spectra * mask_float[:, :, None]
    stacked = spectra.reshape(owned, W, 2, F).transpose(3, 0, 2, 1).reshape(F, owned, 2 * W)
    left, left_mask = (
        lax.all_gather(stacked, "col", axis=1, tiled=True),
        lax.all_gather(mask_float, "col", axis=0, tiled=True),
    )
    right, right_mask = (
        lax.all_gather(stacked, "row", axis=1, tiled=True),
        lax.all_gather(mask_float, "row", axis=0, tiled=True),
    )
    counts = jnp.dot(left_mask, right_mask.T, preferred_element_type=jnp.float32)
    inverse = 1.0 / jnp.maximum(counts, 1.0)
    across = right.shape[1]
    turned = jnp.concatenate([right[:, :, W:], -right[:, :, :W]], axis=2)
    both = jnp.concatenate([right, turned], axis=1)
    product = jnp.einsum("fiw,fjw->ijf", left, both, preferred_element_type=jnp.float32)
    real_part = (product[:, :across, :] * inverse[:, :, None]).astype(jnp.bfloat16)
    imag_part = (product[:, across:, :] * inverse[:, :, None]).astype(jnp.bfloat16)
    return (real_part, imag_part)


def solution(mesh):
    placed = (
        P(("row", "col"), None, None),
        P(("row", "col")),
        P(("row", "col")),
        P(("row", "col"), None),
    )
    return jax.shard_map(
        per_device,
        mesh=mesh,
        in_specs=placed,
        out_specs=(P("row", "col", None), P("row", "col", None)),
        check_vma=False,
    )
```

profile of v0, /device:TPU:0, one launch (start us, length us, event | category | flops | bytes accessed | tf_op | source)
XLA Modules:
  0.0 255.3 jit_solution(14471646643482685491)
XLA Ops:
  7.8 0.7 compare_select_fusion.10
  8.5 0.1 fusion.21
  8.6 0.2 select_reduce_fusion.2
  8.8 0.1 select_reduce_fusion.1
  8.9 0.7 convert_element_type.55
  9.6 5.2 %all-to-all-start = ((bf16[8,1,2]{2,1,0:T(2,128)(2,1)}), bf16[8,1,2]{2,1,0:T(2,128)(2,1)S(1)}, u32[]{:S(2)}, u32[]{:S(2)}) async-start(bf16[8,1,2]{2,1,0:T(2,128)(2,1)} %convert_element_type.55), calls=%async_computation | async-start | bytes 8192 | tf_op jit(solution)/shard_map/all_to_all | solution.py:58
  14.8 0.1 reduce_sum.55
  14.9 6.4 %gather_fusion = bf16[16,64,3072]{2,1,0:T(8,128)(2,1)} fusion(bf16[16,64,3072]{2,1,0:T(8,128)(2,1)} %param.4, s32[1024]{0:T(1024)S(1)} %pad_clamp_fusion.1), kind=kCustom, calls=%fused_computation | custom fusion | bytes 12582976 | tf_op jit(solution)/shard_map/jit(_take)/gather | solution.py:55
  21.3 6.1 %broadcast_select_fusion = bf16[8,2,64,3072]{3,2,1,0:T(8,128)(2,1)} fusion(bf16[8,2,64,3072]{3,2,1,0:T(8,128)(2,1)} %bitcast.32, pred[8,2]{1,0:T(8,128)(4,1)S(1)} %compare_and_fusion), kind=kLoop, calls=%fused_computation.13 | loop fusion | flops 3145728 | bytes 12582928 | tf_op jit(solution)/shard_map/jit(_take)/select_n | solution.py:55
  27.4 0.0 copy-start.3
  27.4 0.0 all-to-all-done
  27.4 4.9 %all-to-all-start.1 = ((bf16[8,2,64,3072]{3,2,1,0:T(8,128)(2,1)}), bf16[8,2,64,3072]{3,2,1,0:T(8,128)(2,1)}, u32[]{:S(2)}, u32[]{:S(2)}) async-start(bf16[8,2,64,3072]{3,2,1,0:T(8,128)(2,1)} %broadcast_select_fusion), calls=%async_computation.1 | async-start | bytes 12582912 | tf_op jit(solution)/shard_map/all_to_all | solution.py:57
  32.3 0.0 all-gather.3.cloned.1.call-start
  32.3 0.0 copy-done.3
  32.4 21.0 %cosine_convert_fusion = (bf16[3072,384]{1,0:T(8,128)(2,1)}, bf16[3072,384]{1,0:T(8,128)(2,1)}) fusion(s32[384]{0:T(512)S(1)} %iota_add_fusion), kind=kLoop, calls=%fused_computation.21 | loop fusion | flops 14155776 | bytes 4720128 | tf_op jit(solution)/shard_map/convert.5
  53.4 0.1 reshape.118
  53.4 0.1 select_reduce_fusion.3
  53.6 0.1 broadcast_in_dim.85
  53.6 0.1 broadcast_in_dim.86
  53.7 50.1 %all-to-all-done.1 = bf16[8,2,64,3072]{3,2,1,0:T(8,128)(2,1)} async-done(((bf16[8,2,64,3072]{3,2,1,0:T(8,128)(2,1)}), bf16[8,2,64,3072]{3,2,1,0:T(8,128)(2,1)}, u32[]{:S(2)}, u32[]{:S(2)}) %all-to-all-start.1) | async-done | bytes 6291488 | tf_op jit(solution)/shard_map/all_to_all | solution.py:57
  103.9 3.5 %gather_fusion.1 = bf16[8,64,3072]{2,1,0:T(8,128)(2,1)S(1)} fusion(bf16[16,64,3072]{2,1,0:T(8,128)(2,1)} %bitcast.4, s32[1024]{0:T(1024)S(1)} %pad_clamp_fusion), kind=kCustom, calls=%fused_computation.1 | custom fusion | bytes 6291488 | tf_op jit(solution)/shard_map/jit(_take)/gather | solution.py:64
  107.4 0.0 copy-start.1
  107.4 0.0 copy-start.2
  107.4 0.5 bitcast_select_fusion
  108.0 1.1 copy-done.1
  109.1 0.7 copy-done.2
  109.8 2.6 %fusion.10 = f32[512,768]{1,0:T(8,128)S(1)} fusion(bf16[512,3072]{1,0:T(8,128)(2,1)S(1)} %bitcast_select_fusion, bf16[3072,384]{1,0:T(8,128)(2,1)S(1)} %copy-done.2, bf16[3072,384]{1,0:T(8,128)(2,1)S(1)} %copy-done.1), kind=kOutput, calls=%fused_computation.16 | convolution fusion | flops 2425356288 | bytes 9437184 | tf_op jit(solution)/shard_map/dot_general | solution.py:26
  112.4 0.1 multiply_add_fusion
  112.5 0.3 copy.29
  112.8 0.1 reduce_sum.58
  112.9 0.1 broadcast_in_dim.94
  113.0 0.3 copy.30
  113.3 0.2 multiply_convert_fusion.1
  113.4 0.2 maximum_multiply_fusion
  113.6 1.3 copy.34
  115.0 0.0 all-gather.3.cloned.1.call-update
  115.0 0.0 all-gather.5.cloned.1.call-start
  115.0 0.7 all-gather.5.cloned.1.call-update
  115.7 12.2 %all_gather.15 = bf16[32,64]{1,0:T(8,128)(2,1)S(1)} all-gather(bf16[8,64]{1,0:T(8,128)(2,1)S(1)} %convert_element_type.51), channel_id=1, replica_groups=mesh['row'=4,'col'=8] {'row'}, dimensions={0}, use_global_device_ids=true | all-gather | bytes 5120 | tf_op jit(solution)/shard_map/all_gather | solution.py:75
  128.0 8.2 %all_gather.14 = bf16[64,64]{1,0:T(8,128)(2,1)S(1)} all-gather(bf16[8,64]{1,0:T(8,128)(2,1)S(1)} %convert_element_type.51), channel_id=1, replica_groups=mesh['row'=4,'col'=8] {'col'}, dimensions={0}, use_global_device_ids=true | all-gather | bytes 9216 | tf_op jit(solution)/shard_map/all_gather | solution.py:71
  136.1 0.1 fusion.20
  136.3 41.8 %all-gather.3.cloned.1.call-done = bf16[384,32,128]{2,1,0:T(8,128)(2,1)} async-done(((bf16[384,8,128]{2,1,0:T(8,128)(2,1)}), bf16[384,32,128]{2,1,0:T(8,128)(2,1)}) %all-gather.3.cloned.1.call-update) | async-done | bytes 3145744 | tf_op jit(solution)/shard_map/all_gather | solution.py:74
  178.0 6.7 %fusion.28 = (bf16[384,32,64]{2,1,0:T(8,128)(2,1)}, bf16[384,32,64]{2,1,0:T(8,128)(2,1)}) fusion(bf16[384,32,128]{2,1,0:T(8,128)(2,1)} %all-gather.3.cloned.1.call-done), kind=kLoop, calls=%fused_computation.71 | loop fusion | flops 786432 | bytes 6291456 | tf_op jit(solution)/shard_map/slice | solution.py:80
  184.7 40.6 %all-gather.5.cloned.1.call-done = bf16[384,64,128]{2,1,0:T(8,128)(2,1)} async-done(((bf16[384,8,128]{2,1,0:T(8,128)(2,1)}), bf16[384,64,128]{2,1,0:T(8,128)(2,1)}) %all-gather.5.cloned.1.call-update) | async-done | bytes 6291472 | tf_op jit(solution)/shard_map/all_gather | solution.py:70
  225.3 7.4 %fusion.17 = f32[64,64,384]{0,1,2:T(8,128)S(1)} fusion(bf16[384,64,128]{2,1,0:T(8,128)(2,1)} %all-gather.5.cloned.1.call-done, bf16[384,32,64]{2,1,0:T(8,128)(2,1)} %get-tuple-element.15, bf16[384,32,64]{2,1,0:T(8,128)(2,1)} %get-tuple-element.14, bf16[384,32,128]{2,1,0:T(8,128)(2,1)} %all-gather.3.cloned.1.call-done), kind=kOutput, calls=%fused_computation.26 | convolution fusion | flops 421527552 | bytes 18874368 | tf_op jit(solution)/shard_map/fiw,fjw->ijf/dot_general | solution.py:82
  232.7 3.5 %fusion = (bf16[64,32,384]{0,1,2:T(8,128)(2,1)}, bf16[64,32,384]{0,1,2:T(8,128)(2,1)}) fusion(f32[64,64,384]{0,1,2:T(8,128)S(1)} %fusion.17, f32[64,32]{0,1:T(8,128)S(1)} %fusion.20), kind=kLoop, calls=%fused_computation.4 | loop fusion | flops 3145728 | bytes 9445376 | tf_op jit(solution)/shard_map/convert_element_type | solution.py:84
  236.3 0.0 copy-start
  236.3 6.9 %copy.36 = bf16[64,32,384]{2,1,0:T(8,128)(2,1)} copy(bf16[64,32,384]{0,1,2:T(8,128)(2,1)} %get-tuple-element.13) | data formatting | bytes 3145728
  243.2 0.0 copy-done
  243.2 5.3 %copy.37 = bf16[64,32,384]{2,1,0:T(8,128)(2,1)} copy(bf16[64,32,384]{0,1,2:T(8,128)(2,1)S(1)} %copy-done) | data formatting | bytes 3145728
  (13 shorter events, 0.1 us)
Async XLA Ops:
  9.6 17.8 %all-to-all-start = ((bf16[8,1,2]{2,1,0:T(2,128)(2,1)}), bf16[8,1,2]{2,1,0:T(2,128)(2,1)S(1)}, u32[]{:S(2)}, u32[]{:S(2)}) async-start(bf16[8,1,2]{2,1,0:T(2,128)(2,1)} %convert_element_type.55), calls=%async_computation | async-start | bytes 8192 | tf_op jit(solution)/shard_map/all_to_all | solution.py:58
  27.4 4.9 %copy-start.3 = (s32[8,64]{1,0:T(8,128)S(1)}, s32[8,64]{1,0:T(8,128)}, u32[]{:S(2)}) copy-start(s32[8,64]{1,0:T(8,128)} %param.7) | copy-start | bytes 6148
  27.4 76.5 %all-to-all-start.1 = ((bf16[8,2,64,3072]{3,2,1,0:T(8,128)(2,1)}), bf16[8,2,64,3072]{3,2,1,0:T(8,128)(2,1)}, u32[]{:S(2)}, u32[]{:S(2)}) async-start(bf16[8,2,64,3072]{3,2,1,0:T(8,128)(2,1)} %broadcast_select_fusion), calls=%async_computation.1 | async-start | bytes 12582912 | tf_op jit(solution)/shard_map/all_to_all | solution.py:57
  32.3 145.7 %all-gather.3.cloned.1.call-start = ((), (), s32[]{:S(2)}) async-start(), calls=%async_computation.2 | async-start | bytes 3932160 | tf_op jit(solution)/shard_map/all_gather | solution.py:74
  107.4 1.7 copy-start.1
  107.4 2.4 copy-start.2
  115.0 110.3 %all-gather.5.cloned.1.call-start = ((), (), s32[]{:S(2)}) async-start(), calls=%async_computation.3 | async-start | bytes 7077888 | tf_op jit(solution)/shard_map/all_gather | solution.py:70
  236.3 6.9 %copy-start = (bf16[64,32,384]{0,1,2:T(8,128)(2,1)S(1)}, bf16[64,32,384]{0,1,2:T(8,128)(2,1)}, u32[]{:S(2)}) copy-start(bf16[64,32,384]{0,1,2:T(8,128)(2,1)} %get-tuple-element.12) | copy-start | bytes 4718596
Sparse Core Ops, SparseCore 0:
  115.1 62.8 all-gather.2
  180.5 44.8 all-gather.4
where the time goes:
time: 256 us; the launch traced here: 255 us
  waiting for transfers between devices  133 us (52%)
  other arithmetic  39.6 us (15%)
  local copies, waits for them, and re-layouts  27 us (11%)
  blocking collectives  20.4 us (8%)
  between operations  14.9 us (6%)
  starting transfers between devices  10.1 us (4%)
  matrix products  10.1 us (4%)
    all_to_all x1, waiting for transfers between devices, per_device(): lax.all_to_all(payload, 'col', split_axis=0, concat_axis=0, tiled=True)  50.1 us
    all_gather x1, waiting for transfers between devices, per_device(): lax.all_gather(stacked, 'row', axis=1, tiled=True)  41.8 us
    all_gather x1, waiting for transfers between devices, per_device(): lax.all_gather(stacked, 'col', axis=1, tiled=True)  40.6 us
    another operation x2, other arithmetic  21.1 us
    unnamed x10, local copies, waits for them, and re-layouts  14.1 us
    all_gather x1, blocking collectives, per_device(): lax.all_gather(mask_float, 'row', axis=0, tiled=True)  12.2 us
    all_gather x1, blocking collectives, per_device(): lax.all_gather(mask_float, 'col', axis=0, tiled=True)  8.17 us
    dot_general x1, matrix products, per_device(): jnp.einsum('fiw,fjw->ijf', left, both, preferred_element_type=jnp.float32)  7.4 us
  transfers between devices with their start and end apart: 4, of which 3 were waited for; matrix products, arithmetic and copies ran while one was open for 16% of the time, Pallas kernels for 0%

commit v1 on v0

--- a/solution.py
+++ b/solution.py
@@ -2,6 +2,7 @@
 
 import jax
 import jax.numpy as jnp
+import numpy as np
 from jax import lax
 from jax.sharding import PartitionSpec as P
 
@@ -14,11 +15,11 @@
 
 
 def transform_table():
-    times = jnp.arange(L, dtype=jnp.int32)
-    freqs = jnp.arange(F, dtype=jnp.int32) + F0
+    times = np.arange(L, dtype=np.int64)
+    freqs = np.arange(F, dtype=np.int64) + F0
     phase = times[:, None] * freqs[None, :] % L
-    angle = phase.astype(jnp.float32) * (2.0 * math.pi / L)
-    return jnp.concatenate([jnp.cos(angle), -jnp.sin(angle)], axis=1).astype(jnp.bfloat16)
+    angle = phase.astype(np.float64) * (2.0 * math.pi / L)
+    return np.concatenate([np.cos(angle), -np.sin(angle)], axis=1).astype(jnp.bfloat16)
 
 
 def whiten(segments, table):
@@ -51,20 +52,16 @@
     source = jnp.sum(jnp.where(chosen, slot_index[None, :], 0), axis=1)
     local_id = jnp.sum(jnp.where(chosen, slot_station[None, :] % owned + 1, 0), axis=1) - 1
     labels = local_id.astype(jnp.bfloat16).reshape(columns, CAP)
-    table = transform_table()
-    payload = jnp.take(recorded, source, axis=0).reshape(columns, CAP, W, L)
-    arrived, tags = (
-        lax.all_to_all(payload, "col", split_axis=0, concat_axis=0, tiled=True),
-        lax.all_to_all(labels, "col", split_axis=0, concat_axis=0, tiled=True),
-    )
+    white = whiten(recorded, transform_table())
+    payload = jnp.take(white, source, axis=0, mode="clip").reshape(columns, CAP, W, 2 * F)
+    tags = lax.all_to_all(labels, "col", split_axis=0, concat_axis=0, tiled=True)
+    arrived = lax.all_to_all(payload, "col", split_axis=0, concat_axis=0, tiled=True)
     tags = tags.reshape(outgoing).astype(jnp.int32)
-    flat = arrived.reshape(outgoing, W, arrived.shape[3])
+    flat = arrived.reshape(outgoing, W, 2 * F)
     match = tags[None, :] == jnp.arange(owned, dtype=jnp.int32)[:, None]
     pick = jnp.sum(jnp.where(match, jnp.arange(outgoing, dtype=jnp.int32)[None, :], 0), axis=1)
-    mine = jnp.take(flat, pick, axis=0)
-    spectra = whiten(mine, table)
     mask_float = window_mask.astype(jnp.bfloat16)
-    spectra = spectra * mask_float[:, :, None]
+    spectra = jnp.take(flat, pick, axis=0, mode="clip") * mask_float[:, :, None]
     stacked = spectra.reshape(owned, W, 2, F).transpose(3, 0, 2, 1).reshape(F, owned, 2 * W)
     left, left_mask = (
         lax.all_gather(stacked, "col", axis=1, tiled=True),

time: 256 us -> 202 us (0.79)
  waiting for transfers between devices: 133 us -> 104 us
  other arithmetic: 39.6 us -> 17.1 us
  local copies, waits for them, and re-layouts: 27 us -> 20 us
  matrix products: 10.1 us -> 16.1 us
    all_to_all x1, waiting for transfers between devices: 50.1 us -> 20.7 us  [per_device(): lax.all_to_all(payload, 'col', split_axis=0, concat_axis=0, tiled=True)]
    another operation x2 -> x1, other arithmetic: 21.1 us -> 1.57 us
    gather x2 -> x3, local copies, waits for them, and re-layouts: 9.92 us -> 2.57 us  [the longest x1 1.79 us: per_device(): jnp.take(white, source, axis=0, mode='clip').reshape(columns, CAP, W, 2 * F)]
    select_n x4 -> x0, other arithmetic: 6.63 us -> none  [the longest x2 6.11 us: per_device(): payload = jnp.take(recorded, source, axis=0).reshape(columns, CAP, W, L)]
    dot_general x1, matrix products: 2.61 us -> 8.62 us  [whiten(): jnp.dot(segments.reshape(count * W, L), table, preferred_element_type=jnp...]
    another operation x0 -> x2, local copies, waits for them, and re-layouts: none -> 2.97 us
    unnamed x10 -> x6, local copies, waits for them, and re-layouts: 14.1 us -> 12.2 us
  transfers between devices with their start and end apart: 4 -> 4, of which waited for: 3 -> 3; matrix products, arithmetic and copies ran while one was open for 16% -> 12% of each run, Pallas kernels for 0% -> 0%
where the time goes in v1:
time: 202 us
  waiting for transfers between devices  104 us (51%)
  blocking collectives  20.3 us (10%)
  local copies, waits for them, and re-layouts  20 us (10%)
  other arithmetic  17.1 us (8%)
  matrix products  16.1 us (8%)
  between operations  14.8 us (7%)
  starting transfers between devices  9.45 us (5%)
    all_gather x1, waiting for transfers between devices, per_device(): lax.all_gather(stacked, 'row', axis=1, tiled=True)  41.8 us
    all_gather x1, waiting for transfers between devices, per_device(): lax.all_gather(stacked, 'col', axis=1, tiled=True)  40.6 us
    all_to_all x1, waiting for transfers between devices, per_device(): lax.all_to_all(payload, 'col', split_axis=0, concat_axis=0, tiled=True)  20.7 us
    unnamed x6, local copies, waits for them, and re-layouts  12.2 us
    all_gather x1, blocking collectives, per_device(): lax.all_gather(mask_float, 'row', axis=0, tiled=True)  12.2 us
    dot_general x1, matrix products, whiten(): jnp.dot(segments.reshape(count * W, L), table, preferred_element_type=jnp...  8.62 us
    all_gather x1, blocking collectives, per_device(): lax.all_gather(mask_float, 'col', axis=0, tiled=True)  8.09 us
    dot_general x1, matrix products, per_device(): jnp.einsum('fiw,fjw->ijf', left, both, preferred_element_type=jnp.float32)  7.4 us
  transfers between devices with their start and end apart: 4, of which 3 were waited for; matrix products, arithmetic and copies ran while one was open for 12% of the time, Pallas kernels for 0%

profile of v1, /device:TPU:0, one launch (start us, length us, event | category | flops | bytes accessed | tf_op | source)
XLA Modules:
  0.0 201.8 jit_solution(5644864027827088221)
XLA Ops:
  7.8 0.7 compare_select_fusion.6
  8.5 0.1 fusion.14
  8.6 0.2 select_reduce_fusion.2
  8.8 0.1 select_reduce_fusion
  8.9 0.7 convert_element_type.47
  9.6 5.2 %all-to-all-start.1 = ((bf16[8,1,2]{2,1,0:T(2,128)(2,1)}), bf16[8,1,2]{2,1,0:T(2,128)(2,1)S(1)}, u32[]{:S(2)}, u32[]{:S(2)}) async-start(bf16[8,1,2]{2,1,0:T(2,128)(2,1)} %convert_element_type.47), calls=%async_computation.1 | async-start | bytes 8192 | tf_op jit(solution)/shard_map/all_to_all | solution.py:57
  14.8 8.6 %convolution_bitcast_fusion = f32[1024,768]{0,1:T(8,128)S(1)} fusion(bf16[3072,768]{1,0:T(8,128)(2,1)} %constant.59.clone, bf16[1024,3072]{1,0:T(8,128)(2,1)} %bitcast.33), kind=kOutput, calls=%fused_computation.16 | convolution fusion | flops 4831838208 | bytes 14155776 | tf_op jit(solution)/shard_map/dot_general | solution.py:27
  23.4 1.5 multiply_add_fusion
  24.9 1.6 reduce_sum.45
  26.5 1.6 fusion.11
  28.0 1.5 copy.24
  29.5 1.5 copy.25
  31.0 0.2 pad_maximum_fusion
  31.2 0.0 copy-start.1
  31.2 1.8 gather_fusion
  33.0 0.0 all-to-all-done.1
  33.0 4.2 %all-to-all-start = ((bf16[8,2,64,768]{3,2,1,0:T(8,128)(2,1)}), bf16[8,2,64,768]{3,2,1,0:T(8,128)(2,1)S(1)}, u32[]{:S(2)}, u32[]{:S(2)}) async-start(bf16[8,2,64,768]{3,2,1,0:T(8,128)(2,1)} %bitcast.7), calls=%async_computation | async-start | bytes 3145728 | tf_op jit(solution)/shard_map/all_to_all | solution.py:58
  37.2 0.0 all-gather.3.cloned.1.call-start
  37.2 0.0 copy-done.1
  37.3 0.1 reshape.76
  37.4 0.1 select_reduce_fusion.3
  37.5 20.7 %all-to-all-done = bf16[8,2,64,768]{3,2,1,0:T(8,128)(2,1)S(1)} async-done(((bf16[8,2,64,768]{3,2,1,0:T(8,128)(2,1)}), bf16[8,2,64,768]{3,2,1,0:T(8,128)(2,1)S(1)}, u32[]{:S(2)}, u32[]{:S(2)}) %all-to-all-start) | async-done | bytes 1572896 | tf_op jit(solution)/shard_map/all_to_all | solution.py:58
  58.2 0.6 gather_fusion.1
  58.8 0.2 gather.12
  59.0 0.9 multiply_bitcast_fusion
  60.0 0.1 copy.27
  60.1 1.3 copy.28
  61.4 0.0 all-gather.3.cloned.1.call-update
  61.5 0.0 all-gather.5.cloned.1.call-start
  61.5 0.7 all-gather.5.cloned.1.call-update
  62.2 12.2 %all_gather.15 = bf16[32,64]{1,0:T(8,128)(2,1)S(1)} all-gather(bf16[8,64]{1,0:T(8,128)(2,1)S(1)} %convert_element_type.43), channel_id=1, replica_groups=mesh['row'=4,'col'=8] {'row'}, dimensions={0}, use_global_device_ids=true | all-gather | bytes 5120 | tf_op jit(solution)/shard_map/all_gather | solution.py:72
  74.4 8.1 %all_gather.14 = bf16[64,64]{1,0:T(8,128)(2,1)S(1)} all-gather(bf16[8,64]{1,0:T(8,128)(2,1)S(1)} %convert_element_type.43), channel_id=1, replica_groups=mesh['row'=4,'col'=8] {'col'}, dimensions={0}, use_global_device_ids=true | all-gather | bytes 9216 | tf_op jit(solution)/shard_map/all_gather | solution.py:68
  82.5 0.1 fusion.13
  82.7 41.8 %all-gather.3.cloned.1.call-done = bf16[384,32,128]{2,1,0:T(8,128)(2,1)} async-done(((bf16[384,8,128]{2,1,0:T(8,128)(2,1)}), bf16[384,32,128]{2,1,0:T(8,128)(2,1)}) %all-gather.3.cloned.1.call-update) | async-done | bytes 3145744 | tf_op jit(solution)/shard_map/all_gather | solution.py:71
  124.5 6.7 %fusion.18 = (bf16[384,32,64]{2,1,0:T(8,128)(2,1)}, bf16[384,32,64]{2,1,0:T(8,128)(2,1)}) fusion(bf16[384,32,128]{2,1,0:T(8,128)(2,1)} %all-gather.3.cloned.1.call-done), kind=kLoop, calls=%fused_computation.50 | loop fusion | flops 786432 | bytes 6291456 | tf_op jit(solution)/shard_map/slice | solution.py:77
  131.2 40.6 %all-gather.5.cloned.1.call-done = bf16[384,64,128]{2,1,0:T(8,128)(2,1)} async-done(((bf16[384,8,128]{2,1,0:T(8,128)(2,1)}), bf16[384,64,128]{2,1,0:T(8,128)(2,1)}) %all-gather.5.cloned.1.call-update) | async-done | bytes 6291472 | tf_op jit(solution)/shard_map/all_gather | solution.py:67
  171.8 7.4 %fusion.8 = f32[64,64,384]{0,1,2:T(8,128)S(1)} fusion(bf16[384,64,128]{2,1,0:T(8,128)(2,1)} %all-gather.5.cloned.1.call-done, bf16[384,32,64]{2,1,0:T(8,128)(2,1)} %get-tuple-element.17, bf16[384,32,64]{2,1,0:T(8,128)(2,1)} %get-tuple-element.16, bf16[384,32,128]{2,1,0:T(8,128)(2,1)} %all-gather.3.cloned.1.call-done), kind=kOutput, calls=%fused_computation.12 | convolution fusion | flops 421527552 | bytes 18874368 | tf_op jit(solution)/shard_map/fiw,fjw->ijf/dot_general | solution.py:79
  179.2 3.5 %fusion = (bf16[64,32,384]{0,1,2:T(8,128)(2,1)}, bf16[64,32,384]{0,1,2:T(8,128)(2,1)}) fusion(f32[64,64,384]{0,1,2:T(8,128)S(1)} %fusion.8, f32[64,32]{0,1:T(8,128)S(1)} %fusion.13), kind=kLoop, calls=%fused_computation.3 | loop fusion | flops 3145728 | bytes 9445376 | tf_op jit(solution)/shard_map/convert_element_type | solution.py:81
  182.7 0.0 copy-start
  182.7 6.9 %copy.30 = bf16[64,32,384]{2,1,0:T(8,128)(2,1)} copy(bf16[64,32,384]{0,1,2:T(8,128)(2,1)} %get-tuple-element.13) | data formatting | bytes 3145728
  189.7 0.0 copy-done
  189.7 5.3 %copy.31 = bf16[64,32,384]{2,1,0:T(8,128)(2,1)} copy(bf16[64,32,384]{0,1,2:T(8,128)(2,1)S(1)} %copy-done) | data formatting | bytes 3145728
  (8 shorter events, 0.1 us)
Async XLA Ops:
  9.6 23.4 %all-to-all-start.1 = ((bf16[8,1,2]{2,1,0:T(2,128)(2,1)}), bf16[8,1,2]{2,1,0:T(2,128)(2,1)S(1)}, u32[]{:S(2)}, u32[]{:S(2)}) async-start(bf16[8,1,2]{2,1,0:T(2,128)(2,1)} %convert_element_type.47), calls=%async_computation.1 | async-start | bytes 8192 | tf_op jit(solution)/shard_map/all_to_all | solution.py:57
  31.2 6.1 %copy-start.1 = (s32[8,64]{1,0:T(8,128)S(1)}, s32[8,64]{1,0:T(8,128)}, u32[]{:S(2)}) copy-start(s32[8,64]{1,0:T(8,128)} %param.8) | copy-start | bytes 6148
  33.0 25.2 %all-to-all-start = ((bf16[8,2,64,768]{3,2,1,0:T(8,128)(2,1)}), bf16[8,2,64,768]{3,2,1,0:T(8,128)(2,1)S(1)}, u32[]{:S(2)}, u32[]{:S(2)}) async-start(bf16[8,2,64,768]{3,2,1,0:T(8,128)(2,1)} %bitcast.7), calls=%async_computation | async-start | bytes 3145728 | tf_op jit(solution)/shard_map/all_to_all | solution.py:58
  37.2 87.3 %all-gather.3.cloned.1.call-start = ((), (), s32[]{:S(2)}) async-start(), calls=%async_computation.2 | async-start | bytes 3932160 | tf_op jit(solution)/shard_map/all_gather | solution.py:71
  61.5 110.3 %all-gather.5.cloned.1.call-start = ((), (), s32[]{:S(2)}) async-start(), calls=%async_computation.3 | async-start | bytes 7077888 | tf_op jit(solution)/shard_map/all_gather | solution.py:67
  182.7 6.9 %copy-start = (bf16[64,32,384]{0,1,2:T(8,128)(2,1)S(1)}, bf16[64,32,384]{0,1,2:T(8,128)(2,1)}, u32[]{:S(2)}) copy-start(bf16[64,32,384]{0,1,2:T(8,128)(2,1)} %get-tuple-element.12) | copy-start | bytes 4718596
Sparse Core Ops, SparseCore 0:
  61.6 62.8 all-gather.2
  126.9 44.8 all-gather.4

commit v2 on v1

--- a/solution.py
+++ b/solution.py
@@ -1,9 +1,12 @@
+import functools
 import math
 
 import jax
 import jax.numpy as jnp
 import numpy as np
 from jax import lax
+from jax.experimental import pallas as pl
+from jax.experimental.pallas import tpu as pltpu
 from jax.sharding import PartitionSpec as P
 
 F = 384
@@ -12,6 +15,9 @@
 BAND = 64
 CAP = 2
 W = 64
+CHUNK = 128
+HEAD = 16
+MESH = pl.DeviceIdType.MESH
 
 
 def transform_table():
@@ -32,6 +38,272 @@
     factor = jnp.repeat(factor, BAND, axis=1)
     white = jnp.concatenate([real * factor, imag * factor], axis=1)
     return white.astype(jnp.bfloat16).reshape(count, W, 2 * F)
+
+
+def flipped(value, bit):
+    return value + (1 << bit) * (1 - 2 * ((value // (1 << bit)) % 2))
+
+
+def masked(value, mask):
+    bit = 0
+    while mask >> bit:
+        if (mask >> bit) & 1:
+            value = flipped(value, bit)
+        bit += 1
+    return value
+
+
+def gather_kernel(
+    rows, cols, owned, x_ref, head_ref, real_ref, imag_ref,
+    left, right, turnpad, local_sem, cube_send, cube_recv, up_send, up_recv, down_send, down_recv,
+):
+    row = lax.axis_index("row")
+    col = lax.axis_index("col")
+    bits = cols.bit_length() - 1
+    chunks = F // CHUNK
+    depth = CHUNK * owned
+    stations = cols * owned
+    across = rows * owned
+    orders = ([*range(1, bits), 0], [*range(2, bits), 1, 0])
+
+    def span(chunk, half):
+        first = HEAD + chunk * depth + half * (depth // 2)
+        if half == 0 and chunk == 0:
+            return pl.ds(0, HEAD + depth // 2)
+        return pl.ds(first, depth // 2)
+
+    def whole_span(chunk):
+        if chunk == 0:
+            return pl.ds(0, HEAD + depth)
+        return pl.ds(HEAD + chunk * depth, depth)
+
+    def cube_copies(chunk, stage):
+        copies = []
+        for half in range(2):
+            order = orders[half]
+            partner = flipped(col, order[stage])
+            for member in range(1 << stage):
+                mask = 0
+                for place in range(stage):
+                    if (member >> place) & 1:
+                        mask |= 1 << order[place]
+                block = masked(col, mask)
+                index = (1 << stage) - 1 + member
+                ref = left.at[block, span(chunk, half), :]
+                copies.append(
+                    pltpu.make_async_remote_copy(
+                        src_ref=ref,
+                        dst_ref=ref,
+                        send_sem=cube_send.at[chunk, half, index],
+                        recv_sem=cube_recv.at[chunk, half, index],
+                        device_id=(row, partner),
+                        device_id_type=MESH,
+                    )
+                )
+        return copies
+
+    def line_copy(chunk, stage, up):
+        step = 1 if up else -1
+        block = row - step * stage
+        block = jnp.clip(block, 0, rows - 1)
+        ref = right.at[block, whole_span(chunk), :]
+        send, recv = (up_send, up_recv) if up else (down_send, down_recv)
+        return pltpu.make_async_remote_copy(
+            src_ref=ref,
+            dst_ref=ref,
+            send_sem=send.at[chunk, stage],
+            recv_sem=recv.at[chunk, stage],
+            device_id=(jnp.clip(row + step, 0, rows - 1), col),
+            device_id_type=MESH,
+        )
+
+    def line_arrival(chunk, stage, up):
+        step = 1 if up else -1
+        block = jnp.clip(row - step * (stage + 1), 0, rows - 1)
+        ref = right.at[block, whole_span(chunk), :]
+        send, recv = (up_send, up_recv) if up else (down_send, down_recv)
+        return pltpu.make_async_remote_copy(
+            src_ref=ref,
+            dst_ref=ref,
+            send_sem=send.at[chunk, stage],
+            recv_sem=recv.at[chunk, stage],
+            device_id=(jnp.clip(row + step, 0, rows - 1), col),
+            device_id_type=MESH,
+        )
+
+    def sends(stage, up):
+        if up:
+            return jnp.logical_and(row - stage >= 0, row + 1 < rows)
+        return jnp.logical_and(row + stage < rows, row >= 1)
+
+    def receives(stage, up):
+        if up:
+            return row - 1 - stage >= 0
+        return row + 1 + stage < rows
+
+    def start_cube(chunk, stage):
+        for copy in cube_copies(chunk, stage):
+            copy.start()
+
+    def land_cube(chunk, stage):
+        for copy in cube_copies(chunk, stage):
+            copy.wait_recv()
+
+    def start_line(chunk, stage):
+        for up in (True, False):
+            @pl.when(sends(stage, up))
+            def _():
+                line_copy(chunk, stage, up).start()
+
+    def land_line(chunk, stage):
+        for up in (True, False):
+            @pl.when(receives(stage, up))
+            def _():
+                line_arrival(chunk, stage, up).wait_recv()
+
+    own = []
+    for place, (target, index) in enumerate(((left, col), (right, row))):
+        own.append(
+            pltpu.make_async_copy(head_ref, target.at[index, pl.ds(0, HEAD), :], local_sem.at[place, 0])
+        )
+        own.append(
+            pltpu.make_async_copy(
+                x_ref, target.at[index, pl.ds(HEAD, F * owned), :], local_sem.at[place, 1]
+            )
+        )
+    for copy in own:
+        copy.start()
+
+    barrier = pltpu.get_barrier_semaphore()
+    for bit in range(bits):
+        pl.semaphore_signal(
+            barrier, inc=1, device_id=(row, flipped(col, bit)), device_id_type=MESH
+        )
+
+    @pl.when(row + 1 < rows)
+    def _():
+        pl.semaphore_signal(barrier, inc=1, device_id=(row + 1, col), device_id_type=MESH)
+
+    @pl.when(row >= 1)
+    def _():
+        pl.semaphore_signal(barrier, inc=1, device_id=(row - 1, col), device_id_type=MESH)
+
+    inner = jnp.logical_and(row + 1 < rows, row >= 1)
+    pl.semaphore_wait(barrier, bits + jnp.where(inner, 2, 1))
+
+    for copy in own:
+        copy.wait()
+
+    lane = lax.broadcasted_iota(jnp.int32, (across, 2 * W), 1)
+    sign = jnp.where(lane < W, 1.0, -1.0)
+
+    def inverse_counts():
+        left_mask = jnp.concatenate(
+            [left[c, 0:HEAD, :].astype(jnp.float32)[:owned] for c in range(cols)], axis=0
+        ).astype(jnp.bfloat16)
+        right_mask = jnp.concatenate(
+            [right[r, 0:HEAD, :].astype(jnp.float32)[:owned] for r in range(rows)] * 2, axis=0
+        ).astype(jnp.bfloat16)
+        counts = lax.dot_general(
+            left_mask, right_mask, (((1,), (1,)), ((), ())), preferred_element_type=jnp.float32
+        )
+        return 1.0 / jnp.maximum(counts, 1.0)
+
+    def compute(chunk):
+        inverse = inverse_counts()
+        first = HEAD + chunk * depth
+
+        def pair(index, carry):
+            at = pl.ds(pl.multiple_of(first + index * 2 * owned, 2 * owned), 2 * owned)
+            lefts = [left[c, at, :].astype(jnp.float32) for c in range(cols)]
+            rights = [right[r, at, :].astype(jnp.float32) for r in range(rows)]
+            for which in range(2):
+                rows_of = slice(which * owned, (which + 1) * owned)
+                one = jnp.concatenate([v[rows_of] for v in lefts], axis=0).astype(jnp.bfloat16)
+                plain = jnp.concatenate([v[rows_of] for v in rights], axis=0)
+                turned = pltpu.roll(plain, W, 1) * sign
+                both = jnp.concatenate([plain, turned], axis=0).astype(jnp.bfloat16)
+                product = lax.dot_general(
+                    one, both, (((1,), (1,)), ((), ())), preferred_element_type=jnp.float32
+                )
+                put = pl.multiple_of((index * 2 + which) * stations, stations)
+                turnpad[pl.ds(put, stations), 0 : 2 * across] = product * inverse
+            return carry
+
+        lax.fori_loop(0, CHUNK // 2, pair, 0, unroll=2)
+
+        def station(index, carry):
+            block = turnpad[pl.ds(index, CHUNK, stride=stations), :]
+            block = block.T
+            lanes = pl.ds(chunk * CHUNK, CHUNK)
+            real_ref[index, :, lanes] = block[0:across].astype(jnp.bfloat16)
+            imag_ref[index, :, lanes] = block[across : 2 * across].astype(jnp.bfloat16)
+            return carry
+
+        lax.fori_loop(0, stations, station, 0, unroll=2)
+
+    line_stages = rows - 1
+    stages = max(bits, line_stages)
+    for slot in range(chunks + stages):
+        for stage in range(stages, -1, -1):
+            chunk = slot - stage
+            if chunk < 0 or chunk >= chunks:
+                continue
+            if 1 <= stage <= bits:
+                land_cube(chunk, stage - 1)
+            if stage < bits:
+                start_cube(chunk, stage)
+            if 1 <= stage <= line_stages:
+                land_line(chunk, stage - 1)
+            if stage < line_stages:
+                start_line(chunk, stage)
+        done = slot - stages
+        if 0 <= done < chunks:
+            compute(done)
+
+    for chunk in range(chunks):
+        for stage in range(bits):
+            for copy in cube_copies(chunk, stage):
+                copy.wait_send()
+        for stage in range(line_stages):
+            for up in (True, False):
+                @pl.when(sends(stage, up))
+                def _():
+                    line_copy(chunk, stage, up).wait_send()
+
+
+def cross_spectra(stacked, head, owned):
+    rows = lax.axis_size("row")
+    cols = lax.axis_size("col")
+    stations = cols * owned
+    across = rows * owned
+    chunks = F // CHUNK
+    shape = jax.ShapeDtypeStruct((stations, across, F), jnp.bfloat16)
+    depth = HEAD + F * owned
+    return pl.pallas_call(
+        functools.partial(gather_kernel, rows, cols, owned),
+        out_shape=(shape, shape),
+        in_specs=[pl.BlockSpec(memory_space=pl.ANY)] * 2,
+        out_specs=[pl.BlockSpec(memory_space=pltpu.VMEM)] * 2,
+        scratch_shapes=[
+            pltpu.VMEM((cols, depth, 2 * W), jnp.bfloat16),
+            pltpu.VMEM((rows, depth, 2 * W), jnp.bfloat16),
+            pltpu.VMEM((CHUNK * stations, 2 * W), jnp.float32),
+            pltpu.SemaphoreType.DMA((2, 2)),
+            pltpu.SemaphoreType.DMA((chunks, 2, cols - 1)),
+            pltpu.SemaphoreType.DMA((chunks, 2, cols - 1)),
+            pltpu.SemaphoreType.DMA((chunks, rows - 1)),
+            pltpu.SemaphoreType.DMA((chunks, rows - 1)),
+            pltpu.SemaphoreType.DMA((chunks, rows - 1)),
+            pltpu.SemaphoreType.DMA((chunks, rows - 1)),
+        ],
+        compiler_params=pltpu.CompilerParams(
+            collective_id=0, has_side_effects=True, vmem_limit_bytes=56 * 1024 * 1024
+        ),
+        cost_estimate=pl.CostEstimate(
+            flops=4 * F * stations * across * 2 * W, bytes_accessed=20_000_000, transcendentals=0
+        ),
+    )(stacked, head)
 
 
 def per_device(recorded, seg_count, slot_station, window_mask):
@@ -63,23 +335,8 @@
     mask_float = window_mask.astype(jnp.bfloat16)
     spectra = jnp.take(flat, pick, axis=0, mode="clip") * mask_float[:, :, None]
     stacked = spectra.reshape(owned, W, 2, F).transpose(3, 0, 2, 1).reshape(F, owned, 2 * W)
-    left, left_mask = (
-        lax.all_gather(stacked, "col", axis=1, tiled=True),
-        lax.all_gather(mask_float, "col", axis=0, tiled=True),
-    )
-    right, right_mask = (
-        lax.all_gather(stacked, "row", axis=1, tiled=True),
-        lax.all_gather(mask_float, "row", axis=0, tiled=True),
-    )
-    counts = jnp.dot(left_mask, right_mask.T, preferred_element_type=jnp.float32)
-    inverse = 1.0 / jnp.maximum(counts, 1.0)
-    across = right.shape[1]
-    turned = jnp.concatenate([right[:, :, W:], -right[:, :, :W]], axis=2)
-    both = jnp.concatenate([right, turned], axis=1)
-    product = jnp.einsum("fiw,fjw->ijf", left, both, preferred_element_type=jnp.float32)
-    real_part = (product[:, :across, :] * inverse[:, :, None]).astype(jnp.bfloat16)
-    imag_part = (product[:, across:, :] * inverse[:, :, None]).astype(jnp.bfloat16)
-    return (real_part, imag_part)
+    head = jnp.pad(mask_float, ((0, HEAD - owned), (0, W)))
+    return cross_spectra(stacked.reshape(F * owned, 2 * W), head, owned)
 
 
 def solution(mesh):

time: 202 us -> 138 us (0.68)
  waiting for transfers between devices: 104 us -> 20.2 us
  Pallas kernels: 0 us -> 78 us
  blocking collectives: 20.3 us -> 0 us
  between operations: 14.8 us -> 1.4 us
  other arithmetic: 17.1 us -> 6.97 us
  matrix products: 16.1 us -> 8.62 us
  local copies, waits for them, and re-layouts: 20 us -> 13.2 us
    all_gather x2 -> x0, waiting for transfers between devices: 82.4 us -> none  [the longest x1 41.8 us: per_device(): lax.all_gather(stacked, 'row', axis=1, tiled=True)]
    pallas_call x0 -> x1, Pallas kernels: none -> 78 us  [cross_spectra(): pl.pallas_call(functools.partial(gather_kernel, rows, cols, owned), out_s...]
    all_gather x2 -> x0, blocking collectives: 20.3 us -> none  [the longest x1 12.2 us: per_device(): lax.all_gather(mask_float, 'row', axis=0, tiled=True)]
    unnamed x6 -> x8, local copies, waits for them, and re-layouts: 12.2 us -> 3.98 us
    dot_general x2 -> x0, matrix products: 7.52 us -> none  [the longest x1 7.4 us: per_device(): jnp.einsum('fiw,fjw->ijf', left, both, preferred_element_type=jnp.float32)]
    slice x1 -> x0, other arithmetic: 6.68 us -> none  [per_device(): turned = jnp.concatenate([right[:, :, W:], -right[:, :, :W]], axis=2)]
    convert_element_type x1 -> x0, other arithmetic: 3.51 us -> none  [per_device(): (product[:, across:, :] * inverse[:, :, None]).astype(jnp.bfloat16)]
  transfers between devices with their start and end apart: 4 -> 2, of which waited for: 3 -> 1; matrix products, arithmetic and copies ran while one was open for 12% -> 13% of each run, Pallas kernels for 0% -> 0%
where the time goes in v2:
time: 138 us
  Pallas kernels  78 us (57%)
  waiting for transfers between devices  20.2 us (15%)
  local copies, waits for them, and re-layouts  13.2 us (10%)
  starting transfers between devices  9.49 us (7%)
  matrix products  8.62 us (6%)
  other arithmetic  6.97 us (5%)
  between operations  1.4 us (1%)
    pallas_call x1, Pallas kernels, cross_spectra(): pl.pallas_call(functools.partial(gather_kernel, rows, cols, owned), out_s...  78 us
    all_to_all x1, waiting for transfers between devices, per_device(): lax.all_to_all(payload, 'col', split_axis=0, concat_axis=0, tiled=True)  20.2 us
    dot_general x1, matrix products, whiten(): jnp.dot(segments.reshape(count * W, L), table, preferred_element_type=jnp...  8.62 us
    all_to_all x1, starting transfers between devices, per_device(): lax.all_to_all(labels, 'col', split_axis=0, concat_axis=0, tiled=True)  5.17 us
    all_to_all x1, starting transfers between devices, per_device(): lax.all_to_all(payload, 'col', split_axis=0, concat_axis=0, tiled=True)  4.32 us
    unnamed x8, local copies, waits for them, and re-layouts  3.98 us
  transfers between devices with their start and end apart: 2, of which 1 were waited for; matrix products, arithmetic and copies ran while one was open for 13% of the time, Pallas kernels for 0%

profile of v2, /device:TPU:0, one launch (start us, length us, event | category | flops | bytes accessed | tf_op | source)
XLA Modules:
  0.0 137.9 jit_solution(10581073029634390614)
XLA Ops:
  1.3 0.7 compare_select_fusion.6
  1.9 0.1 fusion.2
  2.1 0.2 select_reduce_fusion.2
  2.3 0.1 select_reduce_fusion
  2.4 0.7 convert_element_type.41
  3.1 5.2 %all-to-all-start.1 = ((bf16[8,1,2]{2,1,0:T(2,128)(2,1)}), bf16[8,1,2]{2,1,0:T(2,128)(2,1)S(1)}, u32[]{:S(2)}, u32[]{:S(2)}) async-start(bf16[8,1,2]{2,1,0:T(2,128)(2,1)} %convert_element_type.41), calls=%async_computation.1 | async-start | bytes 8192 | tf_op jit(solution)/shard_map/all_to_all | solution.py:329
  8.2 8.6 %convolution_bitcast_fusion = f32[1024,768]{0,1:T(8,128)S(1)} fusion(bf16[3072,768]{1,0:T(8,128)(2,1)} %constant.59.clone, bf16[1024,3072]{1,0:T(8,128)(2,1)} %bitcast.26), kind=kOutput, calls=%fused_computation.4 | convolution fusion | flops 4831838208 | bytes 14155776 | tf_op jit(solution)/shard_map/dot_general | solution.py:33
  16.9 1.5 %multiply_add_fusion = f32[1024,384]{0,1:T(8,128)} fusion(f32[1024,768]{0,1:T(8,128)S(1)} %convolution_bitcast_fusion), kind=kLoop, calls=%fused_computation.8 | loop fusion | flops 1179648 | bytes 4718592 | tf_op jit(solution)/shard_map/add | solution.py:36
  18.3 1.6 %reduce_sum.45 = f32[1024,6]{0,1:T(8,128)S(1)} reduce(f32[1024,6,64]{0,2,1:T(8,128)} %bitcast.22, f32[]{:T(128)} %constant.47.clone.1), dimensions={2}, to_apply=%region_0.1 | reduce | flops 387072 | bytes 1597444 | tf_op jit(solution)/shard_map/reduce_sum | solution.py:37
  19.9 1.6 %fusion = (bf16[1024,384]{0,1:T(8,128)(2,1)}, bf16[1024,384]{0,1:T(8,128)(2,1)}) fusion(f32[1024,768]{0,1:T(8,128)S(1)} %convolution_bitcast_fusion, f32[1024,6]{0,1:T(8,128)S(1)} %add_rsqrt_fusion), kind=kLoop, calls=%fused_computation.5 | loop fusion | flops 1572864 | bytes 4743168 | tf_op jit(solution)/shard_map/convert.4
  21.5 0.0 copy-start
  21.5 1.6 %copy.15 = bf16[1024,384]{1,0:T(8,128)(2,1)S(1)} copy(bf16[1024,384]{0,1:T(8,128)(2,1)} %get-tuple-element.5) | data formatting | bytes 1572864 | tf_op jit(solution)/shard_map/convert.3
  23.1 0.0 copy-done
  23.1 0.4 copy.14
  23.4 0.2 pad_maximum_fusion
  23.6 1.8 %gather_fusion = bf16[16,64,768]{2,1,0:T(8,128)(2,1)} fusion(bf16[16,64,768]{2,1,0:T(8,128)(2,1)S(1)} %pad_maximum_fusion, s32[1024]{0:T(1024)S(1)} %pad_clamp_fusion.1), kind=kCustom, calls=%fused_computation | custom fusion | bytes 3145792 | tf_op jit(solution)/shard_map/jit(_take)/gather | solution.py:328
  25.4 0.0 all-to-all-done.1
  25.4 0.0 copy-start.2
  25.4 4.3 %all-to-all-start = ((bf16[8,2,64,768]{3,2,1,0:T(8,128)(2,1)}), bf16[8,2,64,768]{3,2,1,0:T(8,128)(2,1)S(1)}, u32[]{:S(2)}, u32[]{:S(2)}) async-start(bf16[8,2,64,768]{3,2,1,0:T(8,128)(2,1)} %bitcast.7), calls=%async_computation | async-start | bytes 3145728 | tf_op jit(solution)/shard_map/all_to_all | solution.py:330
  29.7 0.0 copy-done.2
  29.8 0.6 pad.4.head_ref
  30.4 0.1 reshape.71
  30.5 0.1 select_reduce_fusion.3
  30.6 20.2 %all-to-all-done = bf16[8,2,64,768]{3,2,1,0:T(8,128)(2,1)S(1)} async-done(((bf16[8,2,64,768]{3,2,1,0:T(8,128)(2,1)}), bf16[8,2,64,768]{3,2,1,0:T(8,128)(2,1)S(1)}, u32[]{:S(2)}, u32[]{:S(2)}) %all-to-all-start) | async-done | bytes 1572896 | tf_op jit(solution)/shard_map/all_to_all | solution.py:330
  50.8 0.6 gather_fusion.1
  51.4 0.2 gather.12
  51.6 0.9 multiply_bitcast_fusion
  52.5 1.9 %copy.17 = bf16[384,8,2,64]{3,2,1,0:T(2,128)(2,1)S(1)} copy(bf16[384,8,2,64]{0,2,3,1:T(2,128)(2,1)S(1)} %multiply_bitcast_fusion) | data formatting | bytes 1572864 | tf_op jit(solution)/shard_map/transpose | solution.py:337
  54.4 1.5 %reshape_reshape.3.x_ref = bf16[3072,128]{1,0:T(8,128)(2,1)} reshape(bf16[384,8,2,64]{3,2,1,0:T(2,128)(2,1)S(1)} %copy.17) | data formatting | bytes 1572864 | tf_op jit(solution)/shard_map/reshape;reshape | solution.py:339
  55.9 78.0 %shard_map.68 = (bf16[64,32,384]{2,1,0:T(8,128)(2,1)}, bf16[64,32,384]{2,1,0:T(8,128)(2,1)}) custom-call(bf16[3072,128]{1,0:T(8,128)(2,1)} %reshape_reshape.3.x_ref, bf16[16,128]{1,0:T(8,128)(2,1)} %pad.4.head_ref), custom_call_target="tpu_custom_call" | custom-call | flops 402653184 | bytes 20000000 | tf_op jit(solution)/shard_map/pallas_call | solution.py:283
  133.9 0.0 copy-start.1
  133.9 2.8 %copy.21 = bf16[64,32,384]{2,1,0:T(8,128)(2,1)} copy(bf16[64,32,384]{2,1,0:T(8,128)(2,1)} %get-tuple-element.10) | data formatting | bytes 3145728
  136.7 0.0 copy-done.1
  136.7 1.1 copy.22
  (8 shorter events, 0.1 us)
Async XLA Ops:
  3.1 22.3 %all-to-all-start.1 = ((bf16[8,1,2]{2,1,0:T(2,128)(2,1)}), bf16[8,1,2]{2,1,0:T(2,128)(2,1)S(1)}, u32[]{:S(2)}, u32[]{:S(2)}) async-start(bf16[8,1,2]{2,1,0:T(2,128)(2,1)} %convert_element_type.41), calls=%async_computation.1 | async-start | bytes 8192 | tf_op jit(solution)/shard_map/all_to_all | solution.py:329
  21.5 1.6 %copy-start = (bf16[1024,384]{0,1:T(8,128)(2,1)S(1)}, bf16[1024,384]{0,1:T(8,128)(2,1)}, u32[]{:S(2)}) copy-start(bf16[1024,384]{0,1:T(8,128)(2,1)} %get-tuple-element.4) | copy-start | bytes 2359300
  25.4 4.3 %copy-start.2 = (s32[8,64]{1,0:T(8,128)S(1)}, s32[8,64]{1,0:T(8,128)}, u32[]{:S(2)}) copy-start(s32[8,64]{1,0:T(8,128)} %param.8) | copy-start | bytes 6148
  25.4 25.4 %all-to-all-start = ((bf16[8,2,64,768]{3,2,1,0:T(8,128)(2,1)}), bf16[8,2,64,768]{3,2,1,0:T(8,128)(2,1)S(1)}, u32[]{:S(2)}, u32[]{:S(2)}) async-start(bf16[8,2,64,768]{3,2,1,0:T(8,128)(2,1)} %bitcast.7), calls=%async_computation | async-start | bytes 3145728 | tf_op jit(solution)/shard_map/all_to_all | solution.py:330
  133.9 2.8 %copy-start.1 = (bf16[64,32,384]{2,1,0:T(8,128)(2,1)S(1)}, bf16[64,32,384]{2,1,0:T(8,128)(2,1)}, u32[]{:S(2)}) copy-start(bf16[64,32,384]{2,1,0:T(8,128)(2,1)} %get-tuple-element.11) | copy-start | bytes 4718596

commit v3 on v2

--- a/solution.py
+++ b/solution.py
@@ -17,6 +17,8 @@
 W = 64
 CHUNK = 128
 HEAD = 16
+GROUP = 8
+BATCH = 4
 MESH = pl.DeviceIdType.MESH
 
 
@@ -28,16 +30,50 @@
     return np.concatenate([np.cos(angle), -np.sin(angle)], axis=1).astype(jnp.bfloat16)
 
 
-def whiten(segments, table):
-    count = segments.shape[0]
-    spectrum = jnp.dot(segments.reshape(count * W, L), table, preferred_element_type=jnp.float32)
+def band_means():
+    band = np.arange(F) // BAND
+    return ((band[:, None] == band[None, :]) / BAND).astype(jnp.bfloat16)
+
+
+def whiten_kernel(source_ref, *refs):
+    segments = jnp.concatenate([ref[0] for ref in refs[:BATCH]], axis=0)
+    table_ref, band_ref, out_ref = refs[BATCH:]
+    spectrum = jnp.dot(segments, table_ref[...], preferred_element_type=jnp.float32)
     real = spectrum[:, :F]
     imag = spectrum[:, F:]
-    power = (real * real + imag * imag).reshape(count * W, F // BAND, BAND)
-    factor = lax.rsqrt(jnp.mean(power, axis=2) + 1e-05)
-    factor = jnp.repeat(factor, BAND, axis=1)
+    power = real * real + imag * imag
+    high = power.astype(jnp.bfloat16)
+    low = (power - high.astype(jnp.float32)).astype(jnp.bfloat16)
+    band = band_ref[...]
+    mean = jnp.dot(high, band, preferred_element_type=jnp.float32) + jnp.dot(
+        low, band, preferred_element_type=jnp.float32
+    )
+    factor = lax.rsqrt(mean + 1e-05)
     white = jnp.concatenate([real * factor, imag * factor], axis=1)
-    return white.astype(jnp.bfloat16).reshape(count, W, 2 * F)
+    out_ref[...] = white.astype(jnp.bfloat16).reshape(BATCH, W, 2 * F)
+
+
+def whiten(recorded, source):
+    outgoing = source.shape[0]
+
+    def picked(place):
+        return pl.BlockSpec((1, W, L), lambda g, src: (src[g * BATCH + place], 0, 0))
+
+    return pl.pallas_call(
+        whiten_kernel,
+        grid_spec=pltpu.PrefetchScalarGridSpec(
+            num_scalar_prefetch=1,
+            grid=(outgoing // BATCH,),
+            in_specs=[picked(place) for place in range(BATCH)]
+            + [
+                pl.BlockSpec((L, 2 * F), lambda g, src: (0, 0)),
+                pl.BlockSpec((F, F), lambda g, src: (0, 0)),
+            ],
+            out_specs=pl.BlockSpec((BATCH, W, 2 * F), lambda g, src: (g, 0, 0)),
+        ),
+        out_shape=jax.ShapeDtypeStruct((outgoing, W, 2 * F), jnp.bfloat16),
+        compiler_params=pltpu.CompilerParams(vmem_limit_bytes=48 * 1024 * 1024),
+    )(source, *[recorded] * BATCH, jnp.asarray(transform_table()), jnp.asarray(band_means()))
 
 
 def flipped(value, bit):
@@ -196,51 +232,77 @@
 
     lane = lax.broadcasted_iota(jnp.int32, (across, 2 * W), 1)
     sign = jnp.where(lane < W, 1.0, -1.0)
+    empty = jnp.zeros((2 * across, 2 * W), jnp.bfloat16)
+    half_cols = cols // 2
+    half_stations = stations // 2
+    planes = 4 * across // 128
+
+    def paired(lefts, both):
+        low = jnp.concatenate(lefts[:half_cols], axis=0)
+        high = jnp.concatenate(lefts[half_cols:], axis=0)
+        one = jnp.concatenate([low, high], axis=1).astype(jnp.bfloat16)
+        both = both.astype(jnp.bfloat16)
+        wide = jnp.concatenate(
+            [
+                jnp.concatenate([both, empty], axis=1),
+                jnp.concatenate([empty, both], axis=1),
+            ],
+            axis=0,
+        )
+        return lax.dot_general(
+            one, wide, (((1,), (1,)), ((), ())), preferred_element_type=jnp.float32
+        )
 
     def inverse_counts():
-        left_mask = jnp.concatenate(
-            [left[c, 0:HEAD, :].astype(jnp.float32)[:owned] for c in range(cols)], axis=0
-        ).astype(jnp.bfloat16)
-        right_mask = jnp.concatenate(
-            [right[r, 0:HEAD, :].astype(jnp.float32)[:owned] for r in range(rows)] * 2, axis=0
-        ).astype(jnp.bfloat16)
-        counts = lax.dot_general(
-            left_mask, right_mask, (((1,), (1,)), ((), ())), preferred_element_type=jnp.float32
-        )
+        lefts = [left[c, 0:HEAD, :].astype(jnp.float32)[:owned] for c in range(cols)]
+        rights = [right[r, 0:HEAD, :].astype(jnp.float32)[:owned] for r in range(rows)]
+        counts = paired(lefts, jnp.concatenate(rights * 2, axis=0))
         return 1.0 / jnp.maximum(counts, 1.0)
 
     def compute(chunk):
         inverse = inverse_counts()
         first = HEAD + chunk * depth
 
-        def pair(index, carry):
-            at = pl.ds(pl.multiple_of(first + index * 2 * owned, 2 * owned), 2 * owned)
+        def group(index, carry):
+            at = pl.ds(pl.multiple_of(first + index * GROUP * owned, GROUP * owned // 4), GROUP * owned)
             lefts = [left[c, at, :].astype(jnp.float32) for c in range(cols)]
             rights = [right[r, at, :].astype(jnp.float32) for r in range(rows)]
-            for which in range(2):
+            for which in range(GROUP):
                 rows_of = slice(which * owned, (which + 1) * owned)
-                one = jnp.concatenate([v[rows_of] for v in lefts], axis=0).astype(jnp.bfloat16)
                 plain = jnp.concatenate([v[rows_of] for v in rights], axis=0)
                 turned = pltpu.roll(plain, W, 1) * sign
-                both = jnp.concatenate([plain, turned], axis=0).astype(jnp.bfloat16)
-                product = lax.dot_general(
-                    one, both, (((1,), (1,)), ((), ())), preferred_element_type=jnp.float32
+                product = paired(
+                    [v[rows_of] for v in lefts], jnp.concatenate([plain, turned], axis=0)
                 )
-                put = pl.multiple_of((index * 2 + which) * stations, stations)
-                turnpad[pl.ds(put, stations), 0 : 2 * across] = product * inverse
+                put = pl.multiple_of((index * GROUP + which) * half_stations, half_stations)
+                scaled = product * inverse
+                for plane in range(planes):
+                    turnpad[plane, pl.ds(put, half_stations), :] = scaled[
+                        :, plane * 128 : (plane + 1) * 128
+                    ]
             return carry
 
-        lax.fori_loop(0, CHUNK // 2, pair, 0, unroll=2)
+        lax.fori_loop(0, CHUNK // GROUP, group, 0)
 
         def station(index, carry):
-            block = turnpad[pl.ds(index, CHUNK, stride=stations), :]
-            block = block.T
+            block = jnp.concatenate(
+                [
+                    turnpad[plane, pl.ds(index, CHUNK, stride=half_stations), :].T
+                    for plane in range(planes)
+                ],
+                axis=0,
+            )
             lanes = pl.ds(chunk * CHUNK, CHUNK)
-            real_ref[index, :, lanes] = block[0:across].astype(jnp.bfloat16)
-            imag_ref[index, :, lanes] = block[across : 2 * across].astype(jnp.bfloat16)
+            for half in range(2):
+                base = half * 2 * across
+                put = index + half * half_stations
+                real_ref[put, :, lanes] = block[base : base + across].astype(jnp.bfloat16)
+                imag_ref[put, :, lanes] = block[base + across : base + 2 * across].astype(
+                    jnp.bfloat16
+                )
             return carry
 
-        lax.fori_loop(0, stations, station, 0, unroll=2)
+        lax.fori_loop(0, half_stations, station, 0, unroll=4)
 
     line_stages = rows - 1
     stages = max(bits, line_stages)
@@ -288,7 +350,7 @@
         scratch_shapes=[
             pltpu.VMEM((cols, depth, 2 * W), jnp.bfloat16),
             pltpu.VMEM((rows, depth, 2 * W), jnp.bfloat16),
-            pltpu.VMEM((CHUNK * stations, 2 * W), jnp.float32),
+            pltpu.VMEM((4 * across // 128, CHUNK * stations // 2, 128), jnp.float32),
             pltpu.SemaphoreType.DMA((2, 2)),
             pltpu.SemaphoreType.DMA((chunks, 2, cols - 1)),
             pltpu.SemaphoreType.DMA((chunks, 2, cols - 1)),
@@ -324,8 +386,8 @@
     source = jnp.sum(jnp.where(chosen, slot_index[None, :], 0), axis=1)
     local_id = jnp.sum(jnp.where(chosen, slot_station[None, :] % owned + 1, 0), axis=1) - 1
     labels = local_id.astype(jnp.bfloat16).reshape(columns, CAP)
-    white = whiten(recorded, transform_table())
-    payload = jnp.take(white, source, axis=0, mode="clip").reshape(columns, CAP, W, 2 * F)
+    white = whiten(recorded, source.astype(jnp.int32))
+    payload = white.reshape(columns, CAP, W, 2 * F)
     tags = lax.all_to_all(labels, "col", split_axis=0, concat_axis=0, tiled=True)
     arrived = lax.all_to_all(payload, "col", split_axis=0, concat_axis=0, tiled=True)
     tags = tags.reshape(outgoing).astype(jnp.int32)

time: 138 us -> 126 us (0.913)
  matrix products: 8.62 us -> 0 us
  other arithmetic: 6.97 us -> 2.19 us
  Pallas kernels: 78 us -> 82 us
  local copies, waits for them, and re-layouts: 13.2 us -> 10.5 us
    pallas_call x0 -> x1, Pallas kernels: none -> 13.1 us  [whiten(): pl.pallas_call(whiten_kernel, grid_spec=pltpu.PrefetchScalarGridSpec(num_...]
    pallas_call x1, Pallas kernels: 78 us -> 68.9 us  [cross_spectra(): pl.pallas_call(functools.partial(gather_kernel, rows, cols, owned), out_s...]
    dot_general x1 -> x0, matrix products: 8.62 us -> none  [whiten(): jnp.dot(segments.reshape(count * W, L), table, preferred_element_type=jnp...]
    another operation x2 -> x0, local copies, waits for them, and re-layouts: 1.91 us -> none
    gather x1 -> x0, local copies, waits for them, and re-layouts: 1.79 us -> none  [per_device(): jnp.take(white, source, axis=0, mode='clip').reshape(columns, CAP, W, 2 * F)]
    another operation x1 -> x0, other arithmetic: 1.58 us -> none
    reduce_sum x1 -> x0, other arithmetic: 1.58 us -> none  [whiten(): factor = lax.rsqrt(jnp.mean(power, axis=2) + 1e-05)]
    add x1 -> x0, other arithmetic: 1.45 us -> none  [whiten(): power = (real * real + imag * imag).reshape(count * W, F // BAND, BAND)]
  transfers between devices with their start and end apart: 2 -> 2, of which waited for: 1 -> 1; matrix products, arithmetic and copies ran while one was open for 13% -> 1% of each run, Pallas kernels for 0% -> 10%
where the time goes in v3:
time: 126 us
  Pallas kernels  82 us (65%)
  waiting for transfers between devices  20.2 us (16%)
  local copies, waits for them, and re-layouts  10.5 us (8%)
  starting transfers between devices  9.49 us (8%)
  other arithmetic  2.19 us (2%)
  between operations  1.35 us (1%)
    pallas_call x1, Pallas kernels, cross_spectra(): pl.pallas_call(functools.partial(gather_kernel, rows, cols, owned), out_s...  68.9 us
    all_to_all x1, waiting for transfers between devices, per_device(): lax.all_to_all(payload, 'col', split_axis=0, concat_axis=0, tiled=True)  20.2 us
    pallas_call x1, Pallas kernels, whiten(): pl.pallas_call(whiten_kernel, grid_spec=pltpu.PrefetchScalarGridSpec(num_...  13.1 us
    all_to_all x1, starting transfers between devices, per_device(): lax.all_to_all(labels, 'col', split_axis=0, concat_axis=0, tiled=True)  5.17 us
    unnamed x8, local copies, waits for them, and re-layouts  4.93 us
    all_to_all x1, starting transfers between devices, per_device(): lax.all_to_all(payload, 'col', split_axis=0, concat_axis=0, tiled=True)  4.32 us
  transfers between devices with their start and end apart: 2, of which 1 were waited for; matrix products, arithmetic and copies ran while one was open for 1% of the time, Pallas kernels for 10%

profile of v3, /device:TPU:0, one launch (start us, length us, event | category | flops | bytes accessed | tf_op | source)
XLA Modules:
  0.0 125.7 jit_solution(7257137277702767695)
XLA Ops:
  1.3 0.7 compare_select_fusion.6
  1.9 0.1 fusion
  2.1 0.2 select_reduce_fusion.2
  2.3 0.1 select_reduce_fusion
  2.4 0.7 convert_element_type.39
  3.1 5.2 %all-to-all-start.1 = ((bf16[8,1,2]{2,1,0:T(2,128)(2,1)}), bf16[8,1,2]{2,1,0:T(2,128)(2,1)S(1)}, u32[]{:S(2)}, u32[]{:S(2)}) async-start(bf16[8,1,2]{2,1,0:T(2,128)(2,1)} %convert_element_type.39), calls=%async_computation.1 | async-start | bytes 8192 | tf_op jit(solution)/shard_map/all_to_all | solution.py:391
  8.2 0.0 copy-start
  8.2 1.0 copy-done
  9.2 13.1 %shard_map.77 = bf16[16,64,768]{2,1,0:T(8,128)(2,1)} custom-call(s32[16]{0:T(128)S(1)} %get-tuple-element.3.source_ref, bf16[16,64,3072]{2,1,0:T(8,128)(2,1)} %refs_3_.1, bf16[16,64,3072]{2,1,0:T(8,128)(2,1)} %refs_3_.1, bf16[16,64,3072]{2,1,0:T(8,128)(2,1)} %refs_3_.1, bf16[16,64,3072]{2,1,0:T(8,128)(2,1)} %refs_3_.1, ...), custom_call_target="tpu_custom_call" | custom-call | tf_op jit(solution)/shard_map/pallas_call | solution.py:62
  22.3 0.0 all-to-all-done.1
  22.3 0.0 copy-start.2
  22.3 4.3 %all-to-all-start = ((bf16[8,2,64,768]{3,2,1,0:T(8,128)(2,1)}), bf16[8,2,64,768]{3,2,1,0:T(8,128)(2,1)S(1)}, u32[]{:S(2)}, u32[]{:S(2)}) async-start(bf16[8,2,64,768]{3,2,1,0:T(8,128)(2,1)} %bitcast.1), calls=%async_computation | async-start | bytes 3145728 | tf_op jit(solution)/shard_map/all_to_all | solution.py:392
  26.6 0.0 copy-done.2
  26.6 0.6 pad.4.head_ref
  27.3 0.1 reshape.54
  27.3 0.1 select_reduce_fusion.3
  27.5 20.2 %all-to-all-done = bf16[8,2,64,768]{3,2,1,0:T(8,128)(2,1)S(1)} async-done(((bf16[8,2,64,768]{3,2,1,0:T(8,128)(2,1)}), bf16[8,2,64,768]{3,2,1,0:T(8,128)(2,1)S(1)}, u32[]{:S(2)}, u32[]{:S(2)}) %all-to-all-start) | async-done | bytes 1572896 | tf_op jit(solution)/shard_map/all_to_all | solution.py:392
  47.7 0.6 gather_fusion
  48.3 0.2 gather.7
  48.4 0.9 multiply_bitcast_fusion
  49.4 1.9 %copy.12 = bf16[384,8,2,64]{3,2,1,0:T(2,128)(2,1)S(1)} copy(bf16[384,8,2,64]{0,2,3,1:T(2,128)(2,1)S(1)} %multiply_bitcast_fusion) | data formatting | bytes 1572864 | tf_op jit(solution)/shard_map/transpose | solution.py:399
  51.3 1.5 %reshape_reshape.3.x_ref = bf16[3072,128]{1,0:T(8,128)(2,1)} reshape(bf16[384,8,2,64]{3,2,1,0:T(2,128)(2,1)S(1)} %copy.12) | data formatting | bytes 1572864 | tf_op jit(solution)/shard_map/reshape;reshape | solution.py:401
  52.8 68.9 %shard_map.78 = (bf16[64,32,384]{2,1,0:T(8,128)(2,1)}, bf16[64,32,384]{2,1,0:T(8,128)(2,1)}) custom-call(bf16[3072,128]{1,0:T(8,128)(2,1)} %reshape_reshape.3.x_ref, bf16[16,128]{1,0:T(8,128)(2,1)} %pad.4.head_ref), custom_call_target="tpu_custom_call" | custom-call | flops 402653184 | bytes 20000000 | tf_op jit(solution)/shard_map/pallas_call | solution.py:345
  121.7 0.0 copy-start.1
  121.7 2.8 %copy.16 = bf16[64,32,384]{2,1,0:T(8,128)(2,1)} copy(bf16[64,32,384]{2,1,0:T(8,128)(2,1)} %get-tuple-element.8) | data formatting | bytes 3145728
  124.5 0.0 copy-done.1
  124.5 1.1 copy.17
  (6 shorter events, 0.1 us)
Async XLA Ops:
  3.1 19.2 %all-to-all-start.1 = ((bf16[8,1,2]{2,1,0:T(2,128)(2,1)}), bf16[8,1,2]{2,1,0:T(2,128)(2,1)S(1)}, u32[]{:S(2)}, u32[]{:S(2)}) async-start(bf16[8,1,2]{2,1,0:T(2,128)(2,1)} %convert_element_type.39), calls=%async_computation.1 | async-start | bytes 8192 | tf_op jit(solution)/shard_map/all_to_all | solution.py:391
  8.2 1.0 copy-start
  22.3 4.3 %copy-start.2 = (s32[8,64]{1,0:T(8,128)S(1)}, s32[8,64]{1,0:T(8,128)}, u32[]{:S(2)}) copy-start(s32[8,64]{1,0:T(8,128)} %param.9) | copy-start | bytes 6148
  22.3 25.4 %all-to-all-start = ((bf16[8,2,64,768]{3,2,1,0:T(8,128)(2,1)}), bf16[8,2,64,768]{3,2,1,0:T(8,128)(2,1)S(1)}, u32[]{:S(2)}, u32[]{:S(2)}) async-start(bf16[8,2,64,768]{3,2,1,0:T(8,128)(2,1)} %bitcast.1), calls=%async_computation | async-start | bytes 3145728 | tf_op jit(solution)/shard_map/all_to_all | solution.py:392
  121.7 2.8 %copy-start.1 = (bf16[64,32,384]{2,1,0:T(8,128)(2,1)S(1)}, bf16[64,32,384]{2,1,0:T(8,128)(2,1)}, u32[]{:S(2)}) copy-start(bf16[64,32,384]{2,1,0:T(8,128)(2,1)} %get-tuple-element.9) | copy-start | bytes 4718596

commit v4 on v3

--- a/solution.py
+++ b/solution.py
@@ -49,8 +49,12 @@
         low, band, preferred_element_type=jnp.float32
     )
     factor = lax.rsqrt(mean + 1e-05)
-    white = jnp.concatenate([real * factor, imag * factor], axis=1)
-    out_ref[...] = white.astype(jnp.bfloat16).reshape(BATCH, W, 2 * F)
+    real = real * factor
+    imag = imag * factor
+    for chunk in range(F // CHUNK):
+        lanes = slice(chunk * CHUNK, (chunk + 1) * CHUNK)
+        white = jnp.concatenate([real[:, lanes], imag[:, lanes]], axis=1)
+        out_ref[chunk] = white.astype(jnp.bfloat16).reshape(BATCH, W, 2 * CHUNK)
 
 
 def whiten(recorded, source):
@@ -69,9 +73,11 @@
                 pl.BlockSpec((L, 2 * F), lambda g, src: (0, 0)),
                 pl.BlockSpec((F, F), lambda g, src: (0, 0)),
             ],
-            out_specs=pl.BlockSpec((BATCH, W, 2 * F), lambda g, src: (g, 0, 0)),
+            out_specs=pl.BlockSpec(
+                (F // CHUNK, BATCH, W, 2 * CHUNK), lambda g, src: (0, g, 0, 0)
+            ),
         ),
-        out_shape=jax.ShapeDtypeStruct((outgoing, W, 2 * F), jnp.bfloat16),
+        out_shape=jax.ShapeDtypeStruct((F // CHUNK, outgoing, W, 2 * CHUNK), jnp.bfloat16),
         compiler_params=pltpu.CompilerParams(vmem_limit_bytes=48 * 1024 * 1024),
     )(source, *[recorded] * BATCH, jnp.asarray(transform_table()), jnp.asarray(band_means()))
 
@@ -90,8 +96,8 @@
 
 
 def gather_kernel(
-    rows, cols, owned, x_ref, head_ref, real_ref, imag_ref,
-    left, right, turnpad, local_sem, cube_send, cube_recv, up_send, up_recv, down_send, down_recv,
+    rows, cols, owned, white_ref, tag_ref, head_ref, mask_ref, real_ref, imag_ref,
+    left, right, turnpad, arrived, tags, mixed, local_sem, swap_send, swap_recv, tag_send, tag_recv, cube_send, cube_recv, up_send, up_recv, down_send, down_recv,
 ):
     row = lax.axis_index("row")
     col = lax.axis_index("col")
@@ -202,18 +208,20 @@
         own.append(
             pltpu.make_async_copy(head_ref, target.at[index, pl.ds(0, HEAD), :], local_sem.at[place, 0])
         )
+    for chunk in range(chunks):
         own.append(
             pltpu.make_async_copy(
-                x_ref, target.at[index, pl.ds(HEAD, F * owned), :], local_sem.at[place, 1]
+                white_ref.at[chunk, col], arrived.at[chunk, col], local_sem.at[2, chunk]
             )
         )
+    own.append(pltpu.make_async_copy(tag_ref.at[col], tags.at[col], local_sem.at[0, 1]))
     for copy in own:
         copy.start()
 
     barrier = pltpu.get_barrier_semaphore()
-    for bit in range(bits):
+    for member in range(1, cols):
         pl.semaphore_signal(
-            barrier, inc=1, device_id=(row, flipped(col, bit)), device_id_type=MESH
+            barrier, inc=1, device_id=(row, masked(col, member)), device_id_type=MESH
         )
 
     @pl.when(row + 1 < rows)
@@ -225,10 +233,62 @@
         pl.semaphore_signal(barrier, inc=1, device_id=(row - 1, col), device_id_type=MESH)
 
     inner = jnp.logical_and(row + 1 < rows, row >= 1)
-    pl.semaphore_wait(barrier, bits + jnp.where(inner, 2, 1))
-
+    pl.semaphore_wait(barrier, cols - 1 + jnp.where(inner, 2, 1))
+
+    def tag_copy(member, landing):
+        partner = masked(col, member)
+        return pltpu.make_async_remote_copy(
+            src_ref=tag_ref.at[partner],
+            dst_ref=tags.at[partner if landing else col],
+            send_sem=tag_send.at[member - 1],
+            recv_sem=tag_recv.at[member - 1],
+            device_id=(row, partner),
+            device_id_type=MESH,
+        )
+
+    def swap_copy(chunk, member, landing):
+        partner = masked(col, member)
+        return pltpu.make_async_remote_copy(
+            src_ref=white_ref.at[chunk, partner],
+            dst_ref=arrived.at[chunk, partner if landing else col],
+            send_sem=swap_send.at[chunk, member - 1],
+            recv_sem=swap_recv.at[chunk, member - 1],
+            device_id=(row, partner),
+            device_id_type=MESH,
+        )
+
+    for member in range(1, cols):
+        tag_copy(member, False).start()
+    for chunk in range(chunks):
+        for member in range(1, cols):
+            swap_copy(chunk, member, False).start()
     for copy in own:
         copy.wait()
+
+    def prepare(chunk):
+        for member in range(1, cols):
+            if chunk == 0:
+                tag_copy(member, True).wait_recv()
+            swap_copy(chunk, member, True).wait_recv()
+        names = [tags[c].astype(jnp.float32) for c in range(cols)]
+        names = [names[c][rank : rank + 1, :] for c in range(cols) for rank in range(CAP)]
+
+        def choose(station, carry):
+            name = station.astype(jnp.float32)
+            total = jnp.zeros((W, 2 * CHUNK), jnp.float32)
+            for slot in range(cols * CAP):
+                weight = jnp.where(names[slot] == name, 1.0, 0.0)
+                weight = jnp.concatenate([weight, weight], axis=1)
+                total += arrived[chunk, slot // CAP, slot % CAP].astype(jnp.float32) * weight
+            both = jnp.concatenate([total[:, :CHUNK], total[:, CHUNK:]], axis=0)
+            mixed[pl.ds(station, CHUNK, stride=owned), :] = both.T * mask_ref[pl.ds(station, 1), :]
+            return carry
+
+        lax.fori_loop(0, owned, choose, 0)
+        block = mixed[...].astype(jnp.bfloat16)
+        at = pl.ds(HEAD + chunk * depth, depth)
+        left[col, at, :] = block
+        right[row, at, :] = block
 
     lane = lax.broadcasted_iota(jnp.int32, (across, 2 * W), 1)
     sign = jnp.where(lane < W, 1.0, -1.0)
@@ -313,6 +373,8 @@
                 continue
             if 1 <= stage <= bits:
                 land_cube(chunk, stage - 1)
+            if stage == 0:
+                prepare(chunk)
             if stage < bits:
                 start_cube(chunk, stage)
             if 1 <= stage <= line_stages:
@@ -323,6 +385,10 @@
         if 0 <= done < chunks:
             compute(done)
 
+    for member in range(1, cols):
+        tag_copy(member, False).wait_send()
+        for chunk in range(chunks):
+            swap_copy(chunk, member, False).wait_send()
     for chunk in range(chunks):
         for stage in range(bits):
             for copy in cube_copies(chunk, stage):
@@ -334,7 +400,7 @@
                     line_copy(chunk, stage, up).wait_send()
 
 
-def cross_spectra(stacked, head, owned):
+def cross_spectra(white, tags, head, mask, owned):
     rows = lax.axis_size("row")
     cols = lax.axis_size("col")
     stations = cols * owned
@@ -345,13 +411,21 @@
     return pl.pallas_call(
         functools.partial(gather_kernel, rows, cols, owned),
         out_shape=(shape, shape),
-        in_specs=[pl.BlockSpec(memory_space=pl.ANY)] * 2,
+        in_specs=[pl.BlockSpec(memory_space=pl.ANY)] * 3
+        + [pl.BlockSpec(memory_space=pltpu.VMEM)],
         out_specs=[pl.BlockSpec(memory_space=pltpu.VMEM)] * 2,
         scratch_shapes=[
             pltpu.VMEM((cols, depth, 2 * W), jnp.bfloat16),
             pltpu.VMEM((rows, depth, 2 * W), jnp.bfloat16),
             pltpu.VMEM((4 * across // 128, CHUNK * stations // 2, 128), jnp.float32),
-            pltpu.SemaphoreType.DMA((2, 2)),
+            pltpu.VMEM((chunks, cols, CAP, W, 2 * CHUNK), jnp.bfloat16),
+            pltpu.VMEM((cols, HEAD, 2 * W), jnp.bfloat16),
+            pltpu.VMEM((CHUNK * owned, 2 * W), jnp.float32),
+            pltpu.SemaphoreType.DMA((3, max(chunks, 2))),
+            pltpu.SemaphoreType.DMA((chunks, cols - 1)),
+            pltpu.SemaphoreType.DMA((chunks, cols - 1)),
+            pltpu.SemaphoreType.DMA((cols - 1,)),
+            pltpu.SemaphoreType.DMA((cols - 1,)),
             pltpu.SemaphoreType.DMA((chunks, 2, cols - 1)),
             pltpu.SemaphoreType.DMA((chunks, 2, cols - 1)),
             pltpu.SemaphoreType.DMA((chunks, rows - 1)),
@@ -365,7 +439,7 @@
         cost_estimate=pl.CostEstimate(
             flops=4 * F * stations * across * 2 * W, bytes_accessed=20_000_000, transcendentals=0
         ),
-    )(stacked, head)
+    )(white, tags, head, mask)
 
 
 def per_device(recorded, seg_count, slot_station, window_mask):
@@ -385,20 +459,14 @@
     chosen = position[None, :] == jnp.arange(outgoing, dtype=jnp.int32)[:, None]
     source = jnp.sum(jnp.where(chosen, slot_index[None, :], 0), axis=1)
     local_id = jnp.sum(jnp.where(chosen, slot_station[None, :] % owned + 1, 0), axis=1) - 1
-    labels = local_id.astype(jnp.bfloat16).reshape(columns, CAP)
+    labels = local_id.astype(jnp.bfloat16).reshape(columns, CAP, 1)
+    labels = jnp.broadcast_to(jnp.pad(labels, ((0, 0), (0, HEAD - CAP), (0, 0))), (columns, HEAD, 2 * W))
     white = whiten(recorded, source.astype(jnp.int32))
-    payload = white.reshape(columns, CAP, W, 2 * F)
-    tags = lax.all_to_all(labels, "col", split_axis=0, concat_axis=0, tiled=True)
-    arrived = lax.all_to_all(payload, "col", split_axis=0, concat_axis=0, tiled=True)
-    tags = tags.reshape(outgoing).astype(jnp.int32)
-    flat = arrived.reshape(outgoing, W, 2 * F)
-    match = tags[None, :] == jnp.arange(owned, dtype=jnp.int32)[:, None]
-    pick = jnp.sum(jnp.where(match, jnp.arange(outgoing, dtype=jnp.int32)[None, :], 0), axis=1)
+    white = white.reshape(F // CHUNK, columns, CAP, W, 2 * CHUNK)
     mask_float = window_mask.astype(jnp.bfloat16)
-    spectra = jnp.take(flat, pick, axis=0, mode="clip") * mask_float[:, :, None]
-    stacked = spectra.reshape(owned, W, 2, F).transpose(3, 0, 2, 1).reshape(F, owned, 2 * W)
     head = jnp.pad(mask_float, ((0, HEAD - owned), (0, W)))
-    return cross_spectra(stacked.reshape(F * owned, 2 * W), head, owned)
+    mask = jnp.concatenate([window_mask, window_mask], axis=1).astype(jnp.float32)
+    return cross_spectra(white, labels, head, mask, owned)
 
 
 def solution(mesh):

time: 126 us -> 112 us (0.89)
  waiting for transfers between devices: 20.2 us -> 0 us
  Pallas kernels: 82 us -> 99.9 us
  starting transfers between devices: 9.49 us -> 0 us
  local copies, waits for them, and re-layouts: 10.5 us -> 7.48 us
    all_to_all x2 -> x0, waiting for transfers between devices: 20.2 us -> none  [the longest x1 20.2 us: per_device(): lax.all_to_all(payload, 'col', split_axis=0, concat_axis=0, tiled=True)]
    pallas_call x1, Pallas kernels: 68.9 us -> 87.4 us  [cross_spectra(): pl.pallas_call(functools.partial(gather_kernel, rows, cols, owned), out_s...]
    all_to_all x2 -> x0, starting transfers between devices: 9.49 us -> none  [the longest x1 5.17 us: per_device(): lax.all_to_all(labels, 'col', split_axis=0, concat_axis=0, tiled=True)]
    transpose x1 -> x0, local copies, waits for them, and re-layouts: 1.94 us -> none  [per_device(): spectra.reshape(owned, W, 2, F).transpose(3, 0, 2, 1)]
    another operation x1 -> x0, local copies, waits for them, and re-layouts: 1.48 us -> none  [per_device(): return cross_spectra(stacked.reshape(F * owned, 2 * W), head, owned)]
    convert_element_type x2, other arithmetic: 0.03 us -> 1.43 us  [the longest x1 1.42 us: per_device(): jnp.concatenate([window_mask, window_mask], axis=1).astype(jnp.float32)]
  transfers between devices with their start and end apart: 2 -> 0, of which waited for: 1 -> 0; matrix products, arithmetic and copies ran while one was open for 1% -> 0% of each run, Pallas kernels for 10% -> 0%
where the time goes in v4:
time: 112 us
  Pallas kernels  99.9 us (89%)
  local copies, waits for them, and re-layouts  7.48 us (7%)
  other arithmetic  3.21 us (3%)
  between operations  1.32 us (1%)
    pallas_call x1, Pallas kernels, cross_spectra(): pl.pallas_call(functools.partial(gather_kernel, rows, cols, owned), out_s...  87.4 us
    pallas_call x1, Pallas kernels, whiten(): pl.pallas_call(whiten_kernel, grid_spec=pltpu.PrefetchScalarGridSpec(num_...  12.6 us
    unnamed x8, local copies, waits for them, and re-layouts  6.07 us

profile of v4, /device:TPU:0, one launch (start us, length us, event | category | flops | bytes accessed | tf_op | source)
XLA Modules:
  0.0 111.9 jit_solution(4562002391654216346)
XLA Ops:
  1.3 0.7 compare_select_fusion.6
  1.9 0.7 convert_element_type.29
  2.6 0.6 pad.9.head_ref
  3.2 1.4 %add_convert_fusion.mask_ref = f32[8,128]{1,0:T(8,128)} fusion(s32[8,64]{1,0:T(8,128)} %param.9), kind=kLoop, calls=%fused_computation.6 | loop fusion | flops 2048 | bytes 6144 | tf_op jit(solution)/shard_map/convert_element_type | solution.py:468
  4.7 0.1 fusion
  4.8 0.2 select_reduce_fusion.2
  5.0 0.1 select_reduce_fusion
  5.1 0.1 convert_element_type.28
  5.2 0.7 broadcast_in_dim.41.tag_ref
  5.9 0.0 copy-start.1
  5.9 1.0 copy-done.1
  6.9 12.6 %shard_map.77 = bf16[3,16,64,256]{3,2,1,0:T(8,128)(2,1)S(1)} custom-call(s32[16]{0:T(128)S(1)} %get-tuple-element.3.source_ref, bf16[16,64,3072]{2,1,0:T(8,128)(2,1)} %refs_3_.1, bf16[16,64,3072]{2,1,0:T(8,128)(2,1)} %refs_3_.1, bf16[16,64,3072]{2,1,0:T(8,128)(2,1)} %refs_3_.1, bf16[16,64,3072]{2,1,0:T(8,128)(2,1)} %refs_3_.1, ...), custom_call_target="tpu_custom_call" | custom-call | tf_op jit(solution)/shard_map/pallas_call | solution.py:66
  19.4 0.0 copy-start
  19.4 1.1 %copy-done = bf16[3,16,64,256]{3,2,1,0:T(8,128)(2,1)} copy-done((bf16[3,16,64,256]{3,2,1,0:T(8,128)(2,1)}, bf16[3,16,64,256]{3,2,1,0:T(8,128)(2,1)S(1)}, u32[]{:S(2)}) %copy-start) | copy-done | bytes 1572888
  20.6 87.4 %shard_map.78 = (bf16[64,32,384]{2,1,0:T(8,128)(2,1)}, bf16[64,32,384]{2,1,0:T(8,128)(2,1)}) custom-call(bf16[3,8,2,64,256]{4,3,2,1,0:T(8,128)(2,1)} %bitcast.6, bf16[8,16,128]{2,1,0:T(8,128)(2,1)} %broadcast_in_dim.41.tag_ref, bf16[16,128]{1,0:T(8,128)(2,1)} %pad.9.head_ref, f32[8,128]{1,0:T(8,128)} %add_convert_fusion.mask_ref), custom_call_target="tpu_custom_call" | custom-call | flops 402653184 | bytes 20000000 | tf_op jit(solution)/shard_map/pallas_call | solution.py:411
  108.0 0.0 copy-start.2
  108.0 2.8 %copy.11 = bf16[64,32,384]{2,1,0:T(8,128)(2,1)} copy(bf16[64,32,384]{2,1,0:T(8,128)(2,1)} %get-tuple-element.8) | data formatting | bytes 3145728
  110.8 0.0 copy-done.2
  110.8 1.1 %copy.12 = bf16[64,32,384]{2,1,0:T(8,128)(2,1)} copy(bf16[64,32,384]{2,1,0:T(8,128)(2,1)S(1)} %copy-done.2) | data formatting | bytes 3145728
  (4 shorter events, 0.1 us)
Async XLA Ops:
  5.9 1.0 copy-start.1
  19.4 1.1 %copy-start = (bf16[3,16,64,256]{3,2,1,0:T(8,128)(2,1)}, bf16[3,16,64,256]{3,2,1,0:T(8,128)(2,1)S(1)}, u32[]{:S(2)}) copy-start(bf16[3,16,64,256]{3,2,1,0:T(8,128)(2,1)S(1)} %shard_map.77) | copy-start | bytes 4718596
  108.0 2.8 %copy-start.2 = (bf16[64,32,384]{2,1,0:T(8,128)(2,1)S(1)}, bf16[64,32,384]{2,1,0:T(8,128)(2,1)}, u32[]{:S(2)}) copy-start(bf16[64,32,384]{2,1,0:T(8,128)(2,1)} %get-tuple-element.9) | copy-start | bytes 4718596

commit v5 on v4

--- a/solution.py
+++ b/solution.py
@@ -18,7 +18,7 @@
 CHUNK = 128
 HEAD = 16
 GROUP = 8
-BATCH = 4
+BATCH = 8
 MESH = pl.DeviceIdType.MESH
 
 
@@ -96,8 +96,8 @@
 
 
 def gather_kernel(
-    rows, cols, owned, white_ref, tag_ref, head_ref, mask_ref, real_ref, imag_ref,
-    left, right, turnpad, arrived, tags, mixed, local_sem, swap_send, swap_recv, tag_send, tag_recv, cube_send, cube_recv, up_send, up_recv, down_send, down_recv,
+    rows, cols, owned, white_ref, tag_ref, mask_ref, real_ref, imag_ref,
+    left, right, turnpad, arrived, tags, mixed, wide_mask, local_sem, swap_send, swap_recv, tag_send, tag_recv, cube_send, cube_recv, up_send, up_recv, down_send, down_recv,
 ):
     row = lax.axis_index("row")
     col = lax.axis_index("col")
@@ -113,11 +113,6 @@
         if half == 0 and chunk == 0:
             return pl.ds(0, HEAD + depth // 2)
         return pl.ds(first, depth // 2)
-
-    def whole_span(chunk):
-        if chunk == 0:
-            return pl.ds(0, HEAD + depth)
-        return pl.ds(HEAD + chunk * depth, depth)
 
     def cube_copies(chunk, stage):
         copies = []
@@ -144,31 +139,31 @@
                 )
         return copies
 
-    def line_copy(chunk, stage, up):
+    def line_copy(chunk, stage, up, half):
         step = 1 if up else -1
         block = row - step * stage
         block = jnp.clip(block, 0, rows - 1)
-        ref = right.at[block, whole_span(chunk), :]
+        ref = right.at[block, span(chunk, half), :]
         send, recv = (up_send, up_recv) if up else (down_send, down_recv)
         return pltpu.make_async_remote_copy(
             src_ref=ref,
             dst_ref=ref,
-            send_sem=send.at[chunk, stage],
-            recv_sem=recv.at[chunk, stage],
+            send_sem=send.at[chunk, half, stage],
+            recv_sem=recv.at[chunk, half, stage],
             device_id=(jnp.clip(row + step, 0, rows - 1), col),
             device_id_type=MESH,
         )
 
-    def line_arrival(chunk, stage, up):
+    def line_arrival(chunk, stage, up, half):
         step = 1 if up else -1
         block = jnp.clip(row - step * (stage + 1), 0, rows - 1)
-        ref = right.at[block, whole_span(chunk), :]
+        ref = right.at[block, span(chunk, half), :]
         send, recv = (up_send, up_recv) if up else (down_send, down_recv)
         return pltpu.make_async_remote_copy(
             src_ref=ref,
             dst_ref=ref,
-            send_sem=send.at[chunk, stage],
-            recv_sem=recv.at[chunk, stage],
+            send_sem=send.at[chunk, half, stage],
+            recv_sem=recv.at[chunk, half, stage],
             device_id=(jnp.clip(row + step, 0, rows - 1), col),
             device_id_type=MESH,
         )
@@ -191,23 +186,19 @@
         for copy in cube_copies(chunk, stage):
             copy.wait_recv()
 
-    def start_line(chunk, stage):
+    def start_line(chunk, stage, half):
         for up in (True, False):
             @pl.when(sends(stage, up))
             def _():
-                line_copy(chunk, stage, up).start()
-
-    def land_line(chunk, stage):
+                line_copy(chunk, stage, up, half).start()
+
+    def land_line(chunk, stage, half):
         for up in (True, False):
             @pl.when(receives(stage, up))
             def _():
-                line_arrival(chunk, stage, up).wait_recv()
+                line_arrival(chunk, stage, up, half).wait_recv()
 
     own = []
-    for place, (target, index) in enumerate(((left, col), (right, row))):
-        own.append(
-            pltpu.make_async_copy(head_ref, target.at[index, pl.ds(0, HEAD), :], local_sem.at[place, 0])
-        )
     for chunk in range(chunks):
         own.append(
             pltpu.make_async_copy(
@@ -259,9 +250,14 @@
 
     for member in range(1, cols):
         tag_copy(member, False).start()
-    for chunk in range(chunks):
-        for member in range(1, cols):
-            swap_copy(chunk, member, False).start()
+    for member in range(1, cols):
+        swap_copy(0, member, False).start()
+    lone = mask_ref[...].astype(jnp.float32)
+    window = jnp.concatenate([lone, lone], axis=1)
+    wide_mask[...] = window
+    header = jnp.concatenate([window, jnp.zeros((HEAD - owned, 2 * W), jnp.float32)], axis=0)
+    left[col, 0:HEAD, :] = header.astype(jnp.bfloat16)
+    right[row, 0:HEAD, :] = header.astype(jnp.bfloat16)
     for copy in own:
         copy.wait()
 
@@ -270,6 +266,9 @@
             if chunk == 0:
                 tag_copy(member, True).wait_recv()
             swap_copy(chunk, member, True).wait_recv()
+        if chunk + 1 < chunks:
+            for member in range(1, cols):
+                swap_copy(chunk + 1, member, False).start()
         names = [tags[c].astype(jnp.float32) for c in range(cols)]
         names = [names[c][rank : rank + 1, :] for c in range(cols) for rank in range(CAP)]
 
@@ -281,7 +280,7 @@
                 weight = jnp.concatenate([weight, weight], axis=1)
                 total += arrived[chunk, slot // CAP, slot % CAP].astype(jnp.float32) * weight
             both = jnp.concatenate([total[:, :CHUNK], total[:, CHUNK:]], axis=0)
-            mixed[pl.ds(station, CHUNK, stride=owned), :] = both.T * mask_ref[pl.ds(station, 1), :]
+            mixed[pl.ds(station, CHUNK, stride=owned), :] = both.T * wide_mask[pl.ds(station, 1), :]
             return carry
 
         lax.fori_loop(0, owned, choose, 0)
@@ -317,7 +316,7 @@
         lefts = [left[c, 0:HEAD, :].astype(jnp.float32)[:owned] for c in range(cols)]
         rights = [right[r, 0:HEAD, :].astype(jnp.float32)[:owned] for r in range(rows)]
         counts = paired(lefts, jnp.concatenate(rights * 2, axis=0))
-        return 1.0 / jnp.maximum(counts, 1.0)
+        return 1.0 / jnp.maximum(0.5 * counts, 1.0)
 
     def compute(chunk):
         inverse = inverse_counts()
@@ -371,16 +370,17 @@
             chunk = slot - stage
             if chunk < 0 or chunk >= chunks:
                 continue
+            if stage == 0:
+                prepare(chunk)
+            for half in range(2):
+                if 1 <= stage <= line_stages:
+                    land_line(chunk, stage - 1, half)
+                if stage < line_stages:
+                    start_line(chunk, stage, half)
             if 1 <= stage <= bits:
                 land_cube(chunk, stage - 1)
-            if stage == 0:
-                prepare(chunk)
             if stage < bits:
                 start_cube(chunk, stage)
-            if 1 <= stage <= line_stages:
-                land_line(chunk, stage - 1)
-            if stage < line_stages:
-                start_line(chunk, stage)
         done = slot - stages
         if 0 <= done < chunks:
             compute(done)
@@ -397,10 +397,11 @@
             for up in (True, False):
                 @pl.when(sends(stage, up))
                 def _():
-                    line_copy(chunk, stage, up).wait_send()
-
-
-def cross_spectra(white, tags, head, mask, owned):
+                    line_copy(chunk, stage, up, 0).wait_send()
+                    line_copy(chunk, stage, up, 1).wait_send()
+
+
+def cross_spectra(white, tags, mask, owned):
     rows = lax.axis_size("row")
     cols = lax.axis_size("col")
     stations = cols * owned
@@ -411,7 +412,7 @@
     return pl.pallas_call(
         functools.partial(gather_kernel, rows, cols, owned),
         out_shape=(shape, shape),
-        in_specs=[pl.BlockSpec(memory_space=pl.ANY)] * 3
+        in_specs=[pl.BlockSpec(memory_space=pl.ANY)] * 2
         + [pl.BlockSpec(memory_space=pltpu.VMEM)],
         out_specs=[pl.BlockSpec(memory_space=pltpu.VMEM)] * 2,
         scratch_shapes=[
@@ -421,6 +422,7 @@
             pltpu.VMEM((chunks, cols, CAP, W, 2 * CHUNK), jnp.bfloat16),
             pltpu.VMEM((cols, HEAD, 2 * W), jnp.bfloat16),
             pltpu.VMEM((CHUNK * owned, 2 * W), jnp.float32),
+            pltpu.VMEM((owned, 2 * W), jnp.float32),
             pltpu.SemaphoreType.DMA((3, max(chunks, 2))),
             pltpu.SemaphoreType.DMA((chunks, cols - 1)),
             pltpu.SemaphoreType.DMA((chunks, cols - 1)),
@@ -428,10 +430,10 @@
             pltpu.SemaphoreType.DMA((cols - 1,)),
             pltpu.SemaphoreType.DMA((chunks, 2, cols - 1)),
             pltpu.SemaphoreType.DMA((chunks, 2, cols - 1)),
-            pltpu.SemaphoreType.DMA((chunks, rows - 1)),
-            pltpu.SemaphoreType.DMA((chunks, rows - 1)),
-            pltpu.SemaphoreType.DMA((chunks, rows - 1)),
-            pltpu.SemaphoreType.DMA((chunks, rows - 1)),
+            pltpu.SemaphoreType.DMA((chunks, 2, rows - 1)),
+            pltpu.SemaphoreType.DMA((chunks, 2, rows - 1)),
+            pltpu.SemaphoreType.DMA((chunks, 2, rows - 1)),
+            pltpu.SemaphoreType.DMA((chunks, 2, rows - 1)),
         ],
         compiler_params=pltpu.CompilerParams(
             collective_id=0, has_side_effects=True, vmem_limit_bytes=56 * 1024 * 1024
@@ -439,7 +441,7 @@
         cost_estimate=pl.CostEstimate(
             flops=4 * F * stations * across * 2 * W, bytes_accessed=20_000_000, transcendentals=0
         ),
-    )(white, tags, head, mask)
+    )(white, tags, mask)
 
 
 def per_device(recorded, seg_count, slot_station, window_mask):
@@ -463,10 +465,7 @@
     labels = jnp.broadcast_to(jnp.pad(labels, ((0, 0), (0, HEAD - CAP), (0, 0))), (columns, HEAD, 2 * W))
     white = whiten(recorded, source.astype(jnp.int32))
     white = white.reshape(F // CHUNK, columns, CAP, W, 2 * CHUNK)
-    mask_float = window_mask.astype(jnp.bfloat16)
-    head = jnp.pad(mask_float, ((0, HEAD - owned), (0, W)))
-    mask = jnp.concatenate([window_mask, window_mask], axis=1).astype(jnp.float32)
-    return cross_spectra(white, labels, head, mask, owned)
+    return cross_spectra(white, labels, window_mask, owned)
 
 
 def solution(mesh):

time: 112 us -> 103 us (0.920)
  Pallas kernels: 99.9 us -> 93.4 us
  other arithmetic: 3.21 us -> 1.1 us
    pallas_call x1, Pallas kernels: 87.4 us -> 80.7 us  [cross_spectra(): pl.pallas_call(functools.partial(gather_kernel, rows, cols, owned), out_s...]
    convert_element_type x2 -> x0, other arithmetic: 2.11 us -> none  [the longest x1 1.42 us: per_device(): jnp.concatenate([window_mask, window_mask], axis=1).astype(jnp.float32)]
where the time goes in v5:
time: 103 us
  Pallas kernels  93.4 us (91%)
  local copies, waits for them, and re-layouts  6.88 us (7%)
  between operations  1.32 us (1%)
  other arithmetic  1.1 us (1%)
    pallas_call x1, Pallas kernels, cross_spectra(): pl.pallas_call(functools.partial(gather_kernel, rows, cols, owned), out_s...  80.7 us
    pallas_call x1, Pallas kernels, whiten(): pl.pallas_call(whiten_kernel, grid_spec=pltpu.PrefetchScalarGridSpec(num_...  12.7 us
    unnamed x8, local copies, waits for them, and re-layouts  6.07 us

profile of v5, /device:TPU:0, one launch (start us, length us, event | category | flops | bytes accessed | tf_op | source)
XLA Modules:
  0.0 102.7 jit_solution(6854710120675134778)
XLA Ops:
  1.3 0.7 compare_select_fusion.6
  1.9 0.1 fusion
  2.1 0.2 select_reduce_fusion.2
  2.3 0.1 select_reduce_fusion
  2.4 0.1 convert_element_type.20
  2.5 0.7 broadcast_in_dim.41.tag_ref
  3.2 0.0 copy-start.1
  3.2 1.0 copy-done.1
  4.2 12.7 %shard_map.77 = bf16[3,16,64,256]{3,2,1,0:T(8,128)(2,1)S(1)} custom-call(s32[16]{0:T(128)S(1)} %get-tuple-element.3.source_ref, bf16[16,64,3072]{2,1,0:T(8,128)(2,1)} %refs_7_.1, bf16[16,64,3072]{2,1,0:T(8,128)(2,1)} %refs_7_.1, bf16[16,64,3072]{2,1,0:T(8,128)(2,1)} %refs_7_.1, bf16[16,64,3072]{2,1,0:T(8,128)(2,1)} %refs_7_.1, ...), custom_call_target="tpu_custom_call" | custom-call | tf_op jit(solution)/shard_map/pallas_call | solution.py:66
  16.8 0.0 copy-start
  16.8 1.1 %copy-done = bf16[3,16,64,256]{3,2,1,0:T(8,128)(2,1)} copy-done((bf16[3,16,64,256]{3,2,1,0:T(8,128)(2,1)}, bf16[3,16,64,256]{3,2,1,0:T(8,128)(2,1)S(1)}, u32[]{:S(2)}) %copy-start) | copy-done | bytes 1572888
  18.0 80.7 %shard_map.78 = (bf16[64,32,384]{2,1,0:T(8,128)(2,1)}, bf16[64,32,384]{2,1,0:T(8,128)(2,1)}) custom-call(bf16[3,8,2,64,256]{4,3,2,1,0:T(8,128)(2,1)} %bitcast.6, bf16[8,16,128]{2,1,0:T(8,128)(2,1)} %broadcast_in_dim.41.tag_ref, s32[8,64]{1,0:T(8,128)} %mask_ref.1), custom_call_target="tpu_custom_call" | custom-call | flops 402653184 | bytes 20000000 | tf_op jit(solution)/shard_map/pallas_call | solution.py:412
  98.7 0.0 copy-start.2
  98.7 2.8 %copy.11 = bf16[64,32,384]{2,1,0:T(8,128)(2,1)} copy(bf16[64,32,384]{2,1,0:T(8,128)(2,1)} %get-tuple-element.8) | data formatting | bytes 3145728
  101.6 0.0 copy-done.2
  101.6 1.1 %copy.12 = bf16[64,32,384]{2,1,0:T(8,128)(2,1)} copy(bf16[64,32,384]{2,1,0:T(8,128)(2,1)S(1)} %copy-done.2) | data formatting | bytes 3145728
  (4 shorter events, 0.1 us)
Async XLA Ops:
  3.2 1.0 copy-start.1
  16.8 1.1 %copy-start = (bf16[3,16,64,256]{3,2,1,0:T(8,128)(2,1)}, bf16[3,16,64,256]{3,2,1,0:T(8,128)(2,1)S(1)}, u32[]{:S(2)}) copy-start(bf16[3,16,64,256]{3,2,1,0:T(8,128)(2,1)S(1)} %shard_map.77) | copy-start | bytes 4718596
  98.7 2.8 %copy-start.2 = (bf16[64,32,384]{2,1,0:T(8,128)(2,1)S(1)}, bf16[64,32,384]{2,1,0:T(8,128)(2,1)}, u32[]{:S(2)}) copy-start(bf16[64,32,384]{2,1,0:T(8,128)(2,1)} %get-tuple-element.9) | copy-start | bytes 4718596

commit v6 on v5

--- a/solution.py
+++ b/solution.py
@@ -19,6 +19,7 @@
 HEAD = 16
 GROUP = 8
 BATCH = 8
+PIECES = 3
 MESH = pl.DeviceIdType.MESH
 
 
@@ -318,7 +319,7 @@
         counts = paired(lefts, jnp.concatenate(rights * 2, axis=0))
         return 1.0 / jnp.maximum(0.5 * counts, 1.0)
 
-    def compute(chunk):
+    def compute(chunk, piece):
         inverse = inverse_counts()
         first = HEAD + chunk * depth
 
@@ -341,7 +342,9 @@
                     ]
             return carry
 
-        lax.fori_loop(0, CHUNK // GROUP, group, 0)
+        steps = CHUNK // GROUP
+        if piece < 2:
+            lax.fori_loop(piece * steps // 2, (piece + 1) * steps // 2, group, 0)
 
         def station(index, carry):
             block = jnp.concatenate(
@@ -361,29 +364,42 @@
                 )
             return carry
 
-        lax.fori_loop(0, half_stations, station, 0, unroll=4)
+        if piece == 2:
+            lax.fori_loop(0, half_stations, station, 0, unroll=4)
 
     line_stages = rows - 1
     stages = max(bits, line_stages)
-    for slot in range(chunks + stages):
-        for stage in range(stages, -1, -1):
-            chunk = slot - stage
-            if chunk < 0 or chunk >= chunks:
-                continue
-            if stage == 0:
-                prepare(chunk)
-            for half in range(2):
-                if 1 <= stage <= line_stages:
-                    land_line(chunk, stage - 1, half)
-                if stage < line_stages:
-                    start_line(chunk, stage, half)
-            if 1 <= stage <= bits:
-                land_cube(chunk, stage - 1)
-            if stage < bits:
-                start_cube(chunk, stage)
-        done = slot - stages
-        if 0 <= done < chunks:
-            compute(done)
+
+    def advance(chunk, stage):
+        for half in range(2):
+            if stage < line_stages:
+                land_line(chunk, stage, half)
+            if stage + 1 < line_stages:
+                start_line(chunk, stage + 1, half)
+        if stage < bits:
+            land_cube(chunk, stage)
+        if stage + 1 < bits:
+            start_cube(chunk, stage + 1)
+
+    def begin(chunk):
+        prepare(chunk)
+        for half in range(2):
+            start_line(chunk, 0, half)
+        start_cube(chunk, 0)
+
+    begin(0)
+    for chunk in range(chunks):
+        for stage in range(stages):
+            if chunk >= 1 and stage < PIECES:
+                compute(chunk - 1, stage)
+            if stage == stages - 1 and chunk + 1 < chunks:
+                begin(chunk + 1)
+            advance(chunk, stage)
+        if chunk >= 1:
+            for piece in range(stages, PIECES):
+                compute(chunk - 1, piece)
+    for piece in range(PIECES):
+        compute(chunks - 1, piece)
 
     for member in range(1, cols):
         tag_copy(member, False).wait_send()

time: 103 us -> 102 us (level)
  Pallas kernels: 93.4 us -> 92 us
    pallas_call x1, Pallas kernels: 80.7 us -> 79.4 us  [cross_spectra(): pl.pallas_call(functools.partial(gather_kernel, rows, cols, owned), out_s...]
where the time goes in v6:
time: 102 us; the launch traced here: 101 us
  Pallas kernels  92 us (90%)
  local copies, waits for them, and re-layouts  6.88 us (7%)
  between operations  1.32 us (1%)
  other arithmetic  1.1 us (1%)
    pallas_call x1, Pallas kernels, cross_spectra(): pl.pallas_call(functools.partial(gather_kernel, rows, cols, owned), out_s...  79.4 us
    pallas_call x1, Pallas kernels, whiten(): pl.pallas_call(whiten_kernel, grid_spec=pltpu.PrefetchScalarGridSpec(num_...  12.7 us
    unnamed x8, local copies, waits for them, and re-layouts  6.07 us

profile of v6, /device:TPU:0, one launch (start us, length us, event | category | flops | bytes accessed | tf_op | source)
XLA Modules:
  0.0 101.3 jit_solution(5367929440792175075)
XLA Ops:
  1.3 0.7 compare_select_fusion.6
  1.9 0.1 fusion
  2.1 0.2 select_reduce_fusion.2
  2.3 0.1 select_reduce_fusion
  2.4 0.1 convert_element_type.20
  2.5 0.7 broadcast_in_dim.41.tag_ref
  3.2 0.0 copy-start.1
  3.2 1.0 copy-done.1
  4.2 12.7 %shard_map.77 = bf16[3,16,64,256]{3,2,1,0:T(8,128)(2,1)S(1)} custom-call(s32[16]{0:T(128)S(1)} %get-tuple-element.3.source_ref, bf16[16,64,3072]{2,1,0:T(8,128)(2,1)} %refs_7_.1, bf16[16,64,3072]{2,1,0:T(8,128)(2,1)} %refs_7_.1, bf16[16,64,3072]{2,1,0:T(8,128)(2,1)} %refs_7_.1, bf16[16,64,3072]{2,1,0:T(8,128)(2,1)} %refs_7_.1, ...), custom_call_target="tpu_custom_call" | custom-call | tf_op jit(solution)/shard_map/pallas_call | solution.py:67
  16.8 0.0 copy-start
  16.8 1.1 %copy-done = bf16[3,16,64,256]{3,2,1,0:T(8,128)(2,1)} copy-done((bf16[3,16,64,256]{3,2,1,0:T(8,128)(2,1)}, bf16[3,16,64,256]{3,2,1,0:T(8,128)(2,1)S(1)}, u32[]{:S(2)}) %copy-start) | copy-done | bytes 1572888
  18.0 79.4 %shard_map.78 = (bf16[64,32,384]{2,1,0:T(8,128)(2,1)}, bf16[64,32,384]{2,1,0:T(8,128)(2,1)}) custom-call(bf16[3,8,2,64,256]{4,3,2,1,0:T(8,128)(2,1)} %bitcast.6, bf16[8,16,128]{2,1,0:T(8,128)(2,1)} %broadcast_in_dim.41.tag_ref, s32[8,64]{1,0:T(8,128)} %mask_ref.1), custom_call_target="tpu_custom_call" | custom-call | flops 402653184 | bytes 20000000 | tf_op jit(solution)/shard_map/pallas_call | solution.py:428
  97.3 0.0 copy-start.2
  97.4 2.8 %copy.11 = bf16[64,32,384]{2,1,0:T(8,128)(2,1)} copy(bf16[64,32,384]{2,1,0:T(8,128)(2,1)} %get-tuple-element.8) | data formatting | bytes 3145728
  100.2 0.0 copy-done.2
  100.2 1.1 %copy.12 = bf16[64,32,384]{2,1,0:T(8,128)(2,1)} copy(bf16[64,32,384]{2,1,0:T(8,128)(2,1)S(1)} %copy-done.2) | data formatting | bytes 3145728
  (4 shorter events, 0.1 us)
Async XLA Ops:
  3.2 1.0 copy-start.1
  16.8 1.1 %copy-start = (bf16[3,16,64,256]{3,2,1,0:T(8,128)(2,1)}, bf16[3,16,64,256]{3,2,1,0:T(8,128)(2,1)S(1)}, u32[]{:S(2)}) copy-start(bf16[3,16,64,256]{3,2,1,0:T(8,128)(2,1)S(1)} %shard_map.77) | copy-start | bytes 4718596
  97.3 2.8 %copy-start.2 = (bf16[64,32,384]{2,1,0:T(8,128)(2,1)S(1)}, bf16[64,32,384]{2,1,0:T(8,128)(2,1)}, u32[]{:S(2)}) copy-start(bf16[64,32,384]{2,1,0:T(8,128)(2,1)} %get-tuple-element.9) | copy-start | bytes 4718596

commit v7 on v6

--- a/solution.py
+++ b/solution.py
@@ -28,33 +28,32 @@
     freqs = np.arange(F, dtype=np.int64) + F0
     phase = times[:, None] * freqs[None, :] % L
     angle = phase.astype(np.float64) * (2.0 * math.pi / L)
-    return np.concatenate([np.cos(angle), -np.sin(angle)], axis=1).astype(jnp.bfloat16)
+    parts = np.stack([np.cos(angle), -np.sin(angle)], axis=1).reshape(L, 2, F // CHUNK, CHUNK)
+    return parts.transpose(0, 2, 1, 3).reshape(L, 2 * F).astype(jnp.bfloat16)
 
 
 def band_means():
-    band = np.arange(F) // BAND
+    band = np.arange(CHUNK) // BAND
     return ((band[:, None] == band[None, :]) / BAND).astype(jnp.bfloat16)
 
 
 def whiten_kernel(source_ref, *refs):
     segments = jnp.concatenate([ref[0] for ref in refs[:BATCH]], axis=0)
     table_ref, band_ref, out_ref = refs[BATCH:]
-    spectrum = jnp.dot(segments, table_ref[...], preferred_element_type=jnp.float32)
-    real = spectrum[:, :F]
-    imag = spectrum[:, F:]
-    power = real * real + imag * imag
-    high = power.astype(jnp.bfloat16)
-    low = (power - high.astype(jnp.float32)).astype(jnp.bfloat16)
     band = band_ref[...]
-    mean = jnp.dot(high, band, preferred_element_type=jnp.float32) + jnp.dot(
-        low, band, preferred_element_type=jnp.float32
-    )
-    factor = lax.rsqrt(mean + 1e-05)
-    real = real * factor
-    imag = imag * factor
     for chunk in range(F // CHUNK):
-        lanes = slice(chunk * CHUNK, (chunk + 1) * CHUNK)
-        white = jnp.concatenate([real[:, lanes], imag[:, lanes]], axis=1)
+        lanes = slice(chunk * 2 * CHUNK, (chunk + 1) * 2 * CHUNK)
+        spectrum = jnp.dot(segments, table_ref[:, lanes], preferred_element_type=jnp.float32)
+        real = spectrum[:, :CHUNK]
+        imag = spectrum[:, CHUNK:]
+        power = real * real + imag * imag
+        high = power.astype(jnp.bfloat16)
+        low = (power - high.astype(jnp.float32)).astype(jnp.bfloat16)
+        mean = jnp.dot(high, band, preferred_element_type=jnp.float32) + jnp.dot(
+            low, band, preferred_element_type=jnp.float32
+        )
+        factor = lax.rsqrt(mean + 1e-05)
+        white = jnp.concatenate([real * factor, imag * factor], axis=1)
         out_ref[chunk] = white.astype(jnp.bfloat16).reshape(BATCH, W, 2 * CHUNK)
 
 
@@ -72,7 +71,7 @@
             in_specs=[picked(place) for place in range(BATCH)]
             + [
                 pl.BlockSpec((L, 2 * F), lambda g, src: (0, 0)),
-                pl.BlockSpec((F, F), lambda g, src: (0, 0)),
+                pl.BlockSpec((CHUNK, CHUNK), lambda g, src: (0, 0)),
             ],
             out_specs=pl.BlockSpec(
                 (F // CHUNK, BATCH, W, 2 * CHUNK), lambda g, src: (0, g, 0, 0)

time: 102 us -> 103 us (level)
  Pallas kernels: 92 us -> 93.3 us
    pallas_call x1, Pallas kernels: 12.7 us -> 14.2 us  [whiten(): pl.pallas_call(whiten_kernel, grid_spec=pltpu.PrefetchScalarGridSpec(num_...]
where the time goes in v7:
time: 103 us; the launch traced here: 102 us
  Pallas kernels  93.3 us (91%)
  local copies, waits for them, and re-layouts  6.68 us (6%)
  between operations  1.32 us (1%)
  other arithmetic  1.1 us (1%)
    pallas_call x1, Pallas kernels, cross_spectra(): pl.pallas_call(functools.partial(gather_kernel, rows, cols, owned), out_s...  79.1 us
    pallas_call x1, Pallas kernels, whiten(): pl.pallas_call(whiten_kernel, grid_spec=pltpu.PrefetchScalarGridSpec(num_...  14.2 us
    unnamed x8, local copies, waits for them, and re-layouts  5.87 us

profile of v7, /device:TPU:0, one launch (start us, length us, event | category | flops | bytes accessed | tf_op | source)
XLA Modules:
  0.0 102.4 jit_solution(17096618972397014525)
XLA Ops:
  1.3 0.7 compare_select_fusion.6
  1.9 0.1 fusion
  2.1 0.2 select_reduce_fusion.2
  2.3 0.1 select_reduce_fusion
  2.4 0.1 convert_element_type.20
  2.5 0.7 broadcast_in_dim.41.tag_ref
  3.2 0.0 copy-start.1
  3.2 0.8 copy-done.1
  4.0 14.2 %shard_map.77 = bf16[3,16,64,256]{3,2,1,0:T(8,128)(2,1)S(1)} custom-call(s32[16]{0:T(128)S(1)} %get-tuple-element.3.source_ref, bf16[16,64,3072]{2,1,0:T(8,128)(2,1)} %refs_7_.1, bf16[16,64,3072]{2,1,0:T(8,128)(2,1)} %refs_7_.1, bf16[16,64,3072]{2,1,0:T(8,128)(2,1)} %refs_7_.1, bf16[16,64,3072]{2,1,0:T(8,128)(2,1)} %refs_7_.1, ...), custom_call_target="tpu_custom_call" | custom-call | tf_op jit(solution)/shard_map/pallas_call | solution.py:66
  18.2 0.0 copy-start
  18.2 1.1 %copy-done = bf16[3,16,64,256]{3,2,1,0:T(8,128)(2,1)} copy-done((bf16[3,16,64,256]{3,2,1,0:T(8,128)(2,1)}, bf16[3,16,64,256]{3,2,1,0:T(8,128)(2,1)S(1)}, u32[]{:S(2)}) %copy-start) | copy-done | bytes 1572888
  19.3 79.1 %shard_map.78 = (bf16[64,32,384]{2,1,0:T(8,128)(2,1)}, bf16[64,32,384]{2,1,0:T(8,128)(2,1)}) custom-call(bf16[3,8,2,64,256]{4,3,2,1,0:T(8,128)(2,1)} %bitcast.6, bf16[8,16,128]{2,1,0:T(8,128)(2,1)} %broadcast_in_dim.41.tag_ref, s32[8,64]{1,0:T(8,128)} %mask_ref.1), custom_call_target="tpu_custom_call" | custom-call | flops 402653184 | bytes 20000000 | tf_op jit(solution)/shard_map/pallas_call | solution.py:427
  98.4 0.0 copy-start.2
  98.4 2.8 %copy.11 = bf16[64,32,384]{2,1,0:T(8,128)(2,1)} copy(bf16[64,32,384]{2,1,0:T(8,128)(2,1)} %get-tuple-element.8) | data formatting | bytes 3145728
  101.2 0.0 copy-done.2
  101.2 1.1 %copy.12 = bf16[64,32,384]{2,1,0:T(8,128)(2,1)} copy(bf16[64,32,384]{2,1,0:T(8,128)(2,1)S(1)} %copy-done.2) | data formatting | bytes 3145728
  (4 shorter events, 0.1 us)
Async XLA Ops:
  3.2 0.8 copy-start.1
  18.2 1.1 %copy-start = (bf16[3,16,64,256]{3,2,1,0:T(8,128)(2,1)}, bf16[3,16,64,256]{3,2,1,0:T(8,128)(2,1)S(1)}, u32[]{:S(2)}) copy-start(bf16[3,16,64,256]{3,2,1,0:T(8,128)(2,1)S(1)} %shard_map.77) | copy-start | bytes 4718596
  98.4 2.8 %copy-start.2 = (bf16[64,32,384]{2,1,0:T(8,128)(2,1)S(1)}, bf16[64,32,384]{2,1,0:T(8,128)(2,1)}, u32[]{:S(2)}) copy-start(bf16[64,32,384]{2,1,0:T(8,128)(2,1)} %get-tuple-element.9) | copy-start | bytes 4718596
